TPU v7x, 128 devices: a whole 4x4x4 slice. The times are simulated.
128 devices in a mesh: gx: 8 (over y, core), gy: 4 (over x), gz: 4 (over z).
Axes of the slice: x: 4, y: 4, z: 4, core: 2. Of those that a mesh axis runs over, the one named last changes fastest.
Arguments:
- velocity: float32 [128, 1024, 512], P('gx', 'gy', 'gz'), may hold values from -6 to 6
Outputs:
- detail_one: float32 [7, 64, 512, 256], P(None, 'gx', 'gy', 'gz')
- detail_two: float32 [7, 32, 256, 128], P(None, 'gx', 'gy', 'gz')
- detail_three: float32 [7, 16, 128, 64], P(None, 'gx', 'gy', 'gz')
- coarse_band: float32 [16, 128, 64], P('gx', 'gy', 'gz')
All inputs are finite; a program needn't handle non-finite values.
Results may differ from a plain program's by a relative error of at most 0.000022.
Values sent between devices are 32-bit elements; how exact they have to be, the bound alone decides.
A program may use at most 64 MiB of HBM per device.

v0:
```python
import math

import jax
import jax.numpy as jnp
from jax import lax
from jax.sharding import PartitionSpec as P

lift_alpha = -1.586134342059924
lift_beta = -0.052980118572961
lift_gamma = 0.882911075530934
lift_delta = 0.443506852043971
scale_low = math.sqrt(2.0) / 1.230174104914001
scale_high = 1.230174104914001 / math.sqrt(2.0)


def extended(cells, sides, width):
    for axis, dim in sides:
        count = lax.axis_size(axis)
        head = lax.slice_in_dim(cells, 0, width, axis=dim)
        tail = lax.slice_in_dim(cells, cells.shape[dim] - width, cells.shape[dim], axis=dim)
        cells = jnp.concatenate(
            [
                lax.ppermute(tail, axis, [(i, (i + 1) % count) for i in range(count)]),
                cells,
                lax.ppermute(head, axis, [((i + 1) % count, i) for i in range(count)]),
            ],
            axis=dim,
        )
    return cells


def take_range(volume, start, stop, axis_dim):
    return lax.slice_in_dim(volume, start, stop, axis=axis_dim)


def split_parity(volume, axis_dim):
    half_len = volume.shape[axis_dim] // 2
    paired = volume.reshape(volume.shape[:axis_dim] + (half_len, 2) + volume.shape[axis_dim + 1 :])
    return (
        lax.index_in_dim(paired, 0, axis_dim + 1, keepdims=False),
        lax.index_in_dim(paired, 1, axis_dim + 1, keepdims=False),
    )


def stack_bands(lowpass, highpass):
    band_count = lowpass.shape[0]
    return jnp.stack([lowpass, highpass], axis=1).reshape((2 * band_count,) + lowpass.shape[1:])


def mirror_pad(volume, axis_dim):
    length = volume.shape[axis_dim]
    head_rows = jnp.flip(take_range(volume, 1, 5, axis_dim), axis=axis_dim)
    tail_rows = jnp.flip(take_range(volume, length - 5, length - 1, axis_dim), axis=axis_dim)
    return jnp.concatenate([head_rows, volume, tail_rows], axis=axis_dim)


def mirror_rims(padded, axis_dim):
    length = padded.shape[axis_dim]
    core_rows = take_range(padded, 4, length - 4, axis_dim)
    mirrored = mirror_pad(core_rows, axis_dim)
    at_start = lax.axis_index("gz") == 0
    at_end = lax.axis_index("gz") == lax.axis_size("gz") - 1
    head_rows = jnp.where(
        at_start, take_range(mirrored, 0, 4, axis_dim), take_range(padded, 0, 4, axis_dim)
    )
    tail_rows = jnp.where(
        at_end,
        take_range(mirrored, length - 4, length, axis_dim),
        take_range(padded, length - 4, length, axis_dim),
    )
    return jnp.concatenate([head_rows, core_rows, tail_rows], axis=axis_dim)


def lift_rimmed(padded, axis_dim):
    evens, odds = split_parity(padded, axis_dim)
    half_len = evens.shape[axis_dim] - 4
    odd_one = take_range(odds, 0, half_len + 3, axis_dim) + lift_alpha * (
        take_range(evens, 0, half_len + 3, axis_dim) + take_range(evens, 1, half_len + 4, axis_dim)
    )
    even_two = take_range(evens, 1, half_len + 3, axis_dim) + lift_beta * (
        take_range(odd_one, 0, half_len + 2, axis_dim)
        + take_range(odd_one, 1, half_len + 3, axis_dim)
    )
    odd_three = take_range(odd_one, 1, half_len + 2, axis_dim) + lift_gamma * (
        take_range(even_two, 0, half_len + 1, axis_dim)
        + take_range(even_two, 1, half_len + 2, axis_dim)
    )
    even_four = take_range(even_two, 1, half_len + 1, axis_dim) + lift_delta * (
        take_range(odd_three, 0, half_len, axis_dim)
        + take_range(odd_three, 1, half_len + 1, axis_dim)
    )
    return (even_four * scale_low, take_range(odd_three, 1, half_len + 1, axis_dim) * scale_high)


def lift_padded(padded):
    for axis_dim in (1, 2, 3):
        padded = stack_bands(*lift_rimmed(padded, axis_dim))
    return padded


def level_sharded(approx):
    bands = approx[None]
    padded = mirror_rims(extended(bands, (("gx", 1), ("gy", 2), ("gz", 3)), 4), 3)
    return lift_padded(padded)


def shards(velocity):
    approx = velocity
    outputs = []
    for level_no in range(3):
        bands = level_sharded(approx)
        approx = bands[0]
        outputs.append(bands[1:])
    return (outputs[0], outputs[1], outputs[2], approx)


def solution(mesh):
    return jax.shard_map(
        shards,
        mesh=mesh,
        in_specs=(P("gx", "gy", "gz"),),
        out_specs=(
            P(None, "gx", "gy", "gz"),
            P(None, "gx", "gy", "gz"),
            P(None, "gx", "gy", "gz"),
            P("gx", "gy", "gz"),
        ),
        check_vma=False,
    )
```

profile of v0, /device:TPU:6, one launch (start us, length us, event | category | flops | bytes accessed | tf_op | source)
XLA Modules:
  0.0 129.3 jit_solution(10919067004577759839)
XLA Ops:
  0.6 1.9 %copy.66 = f32[16,256,128]{1,2,0:T(8,128)S(1)} copy(f32[16,256,128]{2,1,0:T(8,128)} %param.1) | data formatting | bytes 4194304 | tf_op args[0]
  2.7 2.9 %collective-permute-start.1 = (f32[1,4,256,128]{2,3,1,0:T(8,128)S(1)}, f32[1,4,256,128]{2,3,1,0:T(8,128)S(1)}, u32[]{:S(2)}, u32[]{:S(2)}) collective-permute-start(f32[1,4,256,128]{2,3,1,0:T(8,128)S(1)} %get-tuple-element.20), channel_id=1, source_target_pairs={{16,0},{32,16},{48,32},{64,48},{80,64},{96,80},{112,96},{0,112},{1... | collective-permute-start | bytes 1572872 | tf_op jit(solution)/shard_map/ppermute | solution.py:25
  5.6 6.9 %collective-permute-done = f32[1,4,256,128]{2,3,1,0:T(8,128)S(1)} collective-permute-done((f32[1,4,256,128]{2,3,1,0:T(8,128)S(1)}, f32[1,4,256,128]{2,3,1,0:T(8,128)S(1)}, u32[]{:S(2)}, u32[]{:S(2)}) %collective-permute-start) | collective-permute-done | bytes 524320 | tf_op jit(solution)/shard_map/ppermute | solution.py:23
  12.8 2.3 %fusion.92 = (f32[1,24,4,128]{2,3,1,0:T(8,128)}, f32[1,24,4,128]{2,3,1,0:T(8,128)}) fusion(f32[1,24,256,128]{2,3,1,0:T(8,128)S(1)} %pad_maximum_fusion.2), kind=kLoop, calls=%fused_computation.202 | loop fusion | bytes 196608 | tf_op jit(solution)/shard_map/slice | solution.py:20
  15.1 1.9 %copy.67 = f32[1,24,4,128]{3,1,2,0:T(8,128)S(1)} copy(f32[1,24,4,128]{2,3,1,0:T(8,128)} %get-tuple-element.11) | data formatting | bytes 98304 | tf_op jit(solution)/shard_map/slice | solution.py:20
  26.2 1.9 %pad_maximum_fusion.12 = f32[1,24,264,4]{2,3,1,0:T(4,128)} fusion(f32[1,24,4,128]{2,3,1,0:T(8,128)} %copy.70, f32[1,24,4,128]{2,3,1,0:T(8,128)} %copy.69, f32[1,4,256,128]{2,3,1,0:T(8,128)S(1)} %collective-permute-done.1, f32[1,16,256,128]{2,3,1,0:T(8,128)S(1)} %bitcast.112, f32[1,4,256,128]{2,3,1,0:T(8,128)S(1)} %collective-permute-done), kind=kLoop, calls=%fused_computation.118 | loop fusion | flops 101376 | bytes 3345408 | tf_op jit(solution)/shard_map/concatenate | solution.py:21
  28.2 4.1 %collective-permute-start.5 = (f32[1,24,264,4]{2,3,1,0:T(4,128)}, f32[1,24,264,4]{2,3,1,0:T(4,128)}, u32[]{:S(2)}, u32[]{:S(2)}) collective-permute-start(f32[1,24,264,4]{2,3,1,0:T(4,128)} %pad_maximum_fusion.12), channel_id=1, source_target_pairs={{1,0},{2,1},{3,2},{0,3},{5,4},{6,5},{7,6},{4,7},{9,8},{10,9},{11,1... | collective-permute-start | bytes 304136 | tf_op jit(solution)/shard_map/ppermute | solution.py:25
  36.2 5.6 %collective-permute-done.4 = f32[1,24,264,4]{2,3,1,0:T(4,128)S(1)} collective-permute-done((f32[1,24,264,4]{2,3,1,0:T(4,128)}, f32[1,24,264,4]{2,3,1,0:T(4,128)S(1)}, u32[]{:S(2)}, u32[]{:S(2)}) %collective-permute-start.4) | collective-permute-done | bytes 101408 | tf_op jit(solution)/shard_map/ppermute | solution.py:23
  41.8 6.1 %pad_maximum_fusion = f32[1,24,264,136]{2,3,1,0:T(8,128)S(1)} fusion(f32[1,24,264,4]{2,3,1,0:T(4,128)S(1)} %bitcast.139, f32[1,24,4,128]{2,3,1,0:T(8,128)} %copy.70, f32[1,4,256,128]{2,3,1,0:T(8,128)S(1)} %collective-permute-done.1, f32[1,16,256,128]{2,3,1,0:T(8,128)S(1)} %bitcast.114, f32[1,4,256,128]{2,3,1,0:T(8,128)S(1)} %collective-permute-done, ...), kind=kLoop, calls=%fused_computation | loop fusion | flops 5170176 | bytes 6893568 | tf_op jit(solution)/shard_map/concatenate | solution.py:71
  49.0 2.2 %slice_multiply_fusion = (f32[1,8,264,136]{2,3,1,0:T(8,128)}, f32[1,8,264,136]{2,3,1,0:T(8,128)}) fusion(f32[1,9,264,136]{2,3,1,0:T(8,128)S(1)} %fusion.18, f32[1,10,264,136]{2,3,1,0:T(8,128)S(1)} %fusion.16), kind=kLoop, calls=%fused_computation.40 | loop fusion | flops 1436160 | bytes 5744640 | tf_op jit(solution)/shard_map/mul | solution.py:92
  51.1 2.5 %copy.73 = f32[1,8,264,136]{3,1,2,0:T(8,128)S(1)} copy(f32[1,8,264,136]{2,3,1,0:T(8,128)} %get-tuple-element.21) | data formatting | bytes 2297856 | tf_op jit(solution)/shard_map/mul | solution.py:92
  53.7 3.4 %copy.72 = f32[1,8,264,136]{3,1,2,0:T(8,128)} copy(f32[1,8,264,136]{2,3,1,0:T(8,128)} %get-tuple-element.22) | data formatting | bytes 2297856 | tf_op jit(solution)/shard_map/mul | solution.py:92
  57.1 2.0 %fusion.4 = (f32[2,8,132,136]{3,1,2,0:T(8,128)S(1)}, f32[2,8,132,136]{3,1,2,0:T(8,128)S(1)}) fusion(f32[1,8,132,2,136]{4,1,3,2,0:T(8,128)S(1)} %bitcast.120, f32[1,8,132,2,136]{4,1,3,2,0:T(8,128)} %bitcast.121), kind=kLoop, calls=%fused_computation.13 | loop fusion | flops 574464 | bytes 4595712 | tf_op jit(solution)/shard_map/squeeze | solution.py:41
  60.4 2.2 %pad_maximum_fusion.1 = f32[2,2,8,128,136]{4,2,3,0,1:T(8,128)} fusion(f32[2,1,8,128,136]{4,2,3,0,1:T(8,128)S(1)} %get-tuple-element.16, f32[2,1,8,128,136]{4,2,3,0,1:T(8,128)S(1)} %get-tuple-element.15), kind=kLoop, calls=%fused_computation.3 | loop fusion | flops 557056 | bytes 4456448 | tf_op jit(solution)/shard_map/stack | solution.py:47
  62.7 3.9 %copy.74 = f32[2,2,8,128,136]{3,2,4,1,0:T(8,128)S(1)} copy(f32[2,2,8,128,136]{4,2,3,0,1:T(8,128)} %pad_maximum_fusion.1) | data formatting | bytes 4456448 | tf_op jit(solution)/shard_map/stack | solution.py:47
  67.9 2.9 %collective-permute-start.7 = (f32[1,4,128,64]{2,3,1,0:T(8,128)S(1)}, f32[1,4,128,64]{2,3,1,0:T(8,128)S(1)}, u32[]{:S(2)}, u32[]{:S(2)}) collective-permute-start(f32[1,4,128,64]{2,3,1,0:T(8,128)S(1)} %get-tuple-element.18), channel_id=1, source_target_pairs={{16,0},{32,16},{48,32},{64,48},{80,64},{96,80},{112,96},{0,112},{1... | collective-permute-start | bytes 393224 | tf_op jit(solution)/shard_map/ppermute | solution.py:25
  70.9 2.6 %collective-permute-done.6 = f32[1,4,128,64]{2,3,1,0:T(8,128)S(1)} collective-permute-done((f32[1,4,128,64]{2,3,1,0:T(8,128)S(1)}, f32[1,4,128,64]{2,3,1,0:T(8,128)S(1)}, u32[]{:S(2)}, u32[]{:S(2)}) %collective-permute-start.6) | collective-permute-done | bytes 131104 | tf_op jit(solution)/shard_map/ppermute | solution.py:23
  75.9 11.9 %collective-permute-done.8 = f32[1,16,4,64]{2,3,1,0:T(8,128)S(1)} collective-permute-done((f32[1,16,4,64]{2,3,1,0:T(8,128)S(1)}, f32[1,16,4,64]{2,3,1,0:T(8,128)S(1)}, u32[]{:S(2)}, u32[]{:S(2)}) %collective-permute-start.8) | collective-permute-done | bytes 16416 | tf_op jit(solution)/shard_map/ppermute | solution.py:23
  93.6 2.0 %collective-permute-start.10 = (f32[1,16,136,4]{2,3,1,0:T(4,128)}, f32[1,16,136,4]{2,3,1,0:T(4,128)S(1)}, u32[]{:S(2)}, u32[]{:S(2)}) collective-permute-start(f32[1,16,136,4]{2,3,1,0:T(4,128)} %get-tuple-element.23), channel_id=1, source_target_pairs={{0,1},{1,2},{2,3},{3,0},{4,5},{5,6},{6,7},{7,4},{8,9},{9,10},{10,1... | collective-permute-start | bytes 104456 | tf_op jit(solution)/shard_map/ppermute | solution.py:23
  96.5 2.8 %collective-permute-done.10 = f32[1,16,136,4]{2,3,1,0:T(4,128)S(1)} collective-permute-done((f32[1,16,136,4]{2,3,1,0:T(4,128)}, f32[1,16,136,4]{2,3,1,0:T(4,128)S(1)}, u32[]{:S(2)}, u32[]{:S(2)}) %collective-permute-start.10) | collective-permute-done | bytes 34848 | tf_op jit(solution)/shard_map/ppermute | solution.py:23
  100.1 2.4 %pad_maximum_fusion.5 = f32[1,16,136,72]{2,3,1,0:T(8,128)} fusion(f32[1,16,136,4]{2,3,1,0:T(4,128)S(1)} %bitcast.147, f32[1,16,4,64]{2,3,1,0:T(8,128)S(1)} %collective-permute-done.9, f32[1,4,128,64]{2,3,1,0:T(8,128)} %copy-done.2, f32[1,8,128,64]{2,3,1,0:T(8,128)S(1)} %slice.675, f32[1,4,128,64]{2,3,1,0:T(8,128)S(1)} %collective-permute-done.6, ...), kind=kLoop, calls=%fused_computation.41 | loop fusion | flops 940032 | bytes 1253376 | tf_op jit(solution)/shard_map/concatenate | solution.py:71
  108.6 1.9 %collective-permute-done.13 = f32[1,4,64,32]{2,3,1,0:T(8,128)S(1)} collective-permute-done((f32[1,4,64,32]{2,3,1,0:T(8,128)S(1)}, f32[1,4,64,32]{2,3,1,0:T(8,128)S(1)}, u32[]{:S(2)}, u32[]{:S(2)}) %collective-permute-start.13) | collective-permute-done | bytes 32800 | tf_op jit(solution)/shard_map/ppermute | solution.py:25
  110.5 3.0 %collective-permute-done.12 = f32[1,4,64,32]{2,3,1,0:T(8,128)S(1)} collective-permute-done((f32[1,4,64,32]{2,3,1,0:T(8,128)S(1)}, f32[1,4,64,32]{2,3,1,0:T(8,128)S(1)}, u32[]{:S(2)}, u32[]{:S(2)}) %collective-permute-start.12) | collective-permute-done | bytes 32800 | tf_op jit(solution)/shard_map/ppermute | solution.py:23
  121.1 2.1 %collective-permute-start.16 = (f32[1,12,72,4]{2,3,1,0:T(4,128)S(1)}, f32[1,12,72,4]{2,3,1,0:T(4,128)S(1)}, u32[]{:S(2)}, u32[]{:S(2)}) collective-permute-start(f32[1,12,72,4]{2,3,1,0:T(4,128)S(1)} %get-tuple-element.30), channel_id=1, source_target_pairs={{0,1},{1,2},{2,3},{3,0},{4,5},{5,6},{6,7},{7,4},{8,9},{9,10},{10,1... | collective-permute-start | bytes 41480 | tf_op jit(solution)/shard_map/ppermute | solution.py:23
  (127 shorter events, 46.6 us)
Async XLA Ops:
  2.7 9.8 %collective-permute-start = (f32[1,4,256,128]{2,3,1,0:T(8,128)S(1)}, f32[1,4,256,128]{2,3,1,0:T(8,128)S(1)}, u32[]{:S(2)}, u32[]{:S(2)}) collective-permute-start(f32[1,4,256,128]{2,3,1,0:T(8,128)S(1)} %get-tuple-element.19), channel_id=1, source_target_pairs={{0,16},{16,32},{32,48},{48,64},{64,80},{80,96},{96,112},{112,0},{1... | collective-permute-start | bytes 1572872 | tf_op jit(solution)/shard_map/ppermute | solution.py:23
  2.7 9.8 %collective-permute-start.1 = (f32[1,4,256,128]{2,3,1,0:T(8,128)S(1)}, f32[1,4,256,128]{2,3,1,0:T(8,128)S(1)}, u32[]{:S(2)}, u32[]{:S(2)}) collective-permute-start(f32[1,4,256,128]{2,3,1,0:T(8,128)S(1)} %get-tuple-element.20), channel_id=1, source_target_pairs={{16,0},{32,16},{48,32},{64,48},{80,64},{96,80},{112,96},{0,112},{1... | collective-permute-start | bytes 1572872 | tf_op jit(solution)/shard_map/ppermute | solution.py:25
  16.9 4.2 %collective-permute-start.2 = (f32[1,24,4,128]{3,1,2,0:T(8,128)S(1)}, f32[1,24,4,128]{3,1,2,0:T(8,128)S(1)}, u32[]{:S(2)}, u32[]{:S(2)}) collective-permute-start(f32[1,24,4,128]{3,1,2,0:T(8,128)S(1)} %copy.67), channel_id=1, source_target_pairs={{0,4},{4,8},{8,12},{12,0},{1,5},{5,9},{9,13},{13,1},{2,6},{6,10},{... | collective-permute-start | bytes 147464 | tf_op jit(solution)/shard_map/ppermute | solution.py:23
  19.2 5.3 %collective-permute-start.3 = (f32[1,24,4,128]{3,1,2,0:T(8,128)S(1)}, f32[1,24,4,128]{3,1,2,0:T(8,128)S(1)}, u32[]{:S(2)}, u32[]{:S(2)}) collective-permute-start(f32[1,24,4,128]{3,1,2,0:T(8,128)S(1)} %copy.68), channel_id=1, source_target_pairs={{4,0},{8,4},{12,8},{0,12},{5,1},{9,5},{13,9},{1,13},{6,2},{10,6},{... | collective-permute-start | bytes 147464 | tf_op jit(solution)/shard_map/ppermute | solution.py:25
  26.2 6.1 %copy-start = (f32[1,24,4,128]{2,3,1,0:T(8,128)S(1)}, f32[1,24,4,128]{2,3,1,0:T(8,128)}, u32[]{:S(2)}) copy-start(f32[1,24,4,128]{2,3,1,0:T(8,128)} %copy.69) | copy-start | bytes 147460
  26.2 6.1 %copy-start.1 = (f32[1,24,4,128]{2,3,1,0:T(8,128)S(1)}, f32[1,24,4,128]{2,3,1,0:T(8,128)}, u32[]{:S(2)}) copy-start(f32[1,24,4,128]{2,3,1,0:T(8,128)} %copy.70) | copy-start | bytes 147460
  28.2 7.1 %collective-permute-start.5 = (f32[1,24,264,4]{2,3,1,0:T(4,128)}, f32[1,24,264,4]{2,3,1,0:T(4,128)}, u32[]{:S(2)}, u32[]{:S(2)}) collective-permute-start(f32[1,24,264,4]{2,3,1,0:T(4,128)} %pad_maximum_fusion.12), channel_id=1, source_target_pairs={{1,0},{2,1},{3,2},{0,3},{5,4},{6,5},{7,6},{4,7},{9,8},{10,9},{11,1... | collective-permute-start | bytes 304136 | tf_op jit(solution)/shard_map/ppermute | solution.py:25
  35.0 6.8 %collective-permute-start.4 = (f32[1,24,264,4]{2,3,1,0:T(4,128)}, f32[1,24,264,4]{2,3,1,0:T(4,128)S(1)}, u32[]{:S(2)}, u32[]{:S(2)}) collective-permute-start(f32[1,24,264,4]{2,3,1,0:T(4,128)} %get-tuple-element.4), channel_id=1, source_target_pairs={{0,1},{1,2},{2,3},{3,0},{4,5},{5,6},{6,7},{7,4},{8,9},{9,10},{10,1... | collective-permute-start | bytes 304136 | tf_op jit(solution)/shard_map/ppermute | solution.py:23
  67.9 5.6 %collective-permute-start.6 = (f32[1,4,128,64]{2,3,1,0:T(8,128)S(1)}, f32[1,4,128,64]{2,3,1,0:T(8,128)S(1)}, u32[]{:S(2)}, u32[]{:S(2)}) collective-permute-start(f32[1,4,128,64]{2,3,1,0:T(8,128)S(1)} %get-tuple-element.17), channel_id=1, source_target_pairs={{0,16},{16,32},{32,48},{48,64},{64,80},{80,96},{96,112},{112,0},{1... | collective-permute-start | bytes 393224 | tf_op jit(solution)/shard_map/ppermute | solution.py:23
  67.9 5.6 %collective-permute-start.7 = (f32[1,4,128,64]{2,3,1,0:T(8,128)S(1)}, f32[1,4,128,64]{2,3,1,0:T(8,128)S(1)}, u32[]{:S(2)}, u32[]{:S(2)}) collective-permute-start(f32[1,4,128,64]{2,3,1,0:T(8,128)S(1)} %get-tuple-element.18), channel_id=1, source_target_pairs={{16,0},{32,16},{48,32},{64,48},{80,64},{96,80},{112,96},{0,112},{1... | collective-permute-start | bytes 393224 | tf_op jit(solution)/shard_map/ppermute | solution.py:25
  73.5 16.3 %copy-start.2 = (f32[1,4,128,64]{2,3,1,0:T(8,128)}, f32[1,4,128,64]{2,3,1,0:T(8,128)S(1)}, u32[]{:S(2)}) copy-start(f32[1,4,128,64]{2,3,1,0:T(8,128)S(1)} %collective-permute-done.7) | copy-start | bytes 393220
  73.8 14.0 %collective-permute-start.8 = (f32[1,16,4,64]{2,3,1,0:T(8,128)S(1)}, f32[1,16,4,64]{2,3,1,0:T(8,128)S(1)}, u32[]{:S(2)}, u32[]{:S(2)}) collective-permute-start(f32[1,16,4,64]{2,3,1,0:T(8,128)S(1)} %get-tuple-element.37), channel_id=1, source_target_pairs={{0,4},{4,8},{8,12},{12,0},{1,5},{5,9},{9,13},{13,1},{2,6},{6,10},{... | collective-permute-start | bytes 49160 | tf_op jit(solution)/shard_map/ppermute | solution.py:23
  74.1 15.0 %collective-permute-start.9 = (f32[1,16,4,64]{2,3,1,0:T(8,128)S(1)}, f32[1,16,4,64]{2,3,1,0:T(8,128)S(1)}, u32[]{:S(2)}, u32[]{:S(2)}) collective-permute-start(f32[1,16,4,64]{2,3,1,0:T(8,128)S(1)} %get-tuple-element.38), channel_id=1, source_target_pairs={{4,0},{8,4},{12,8},{0,12},{5,1},{9,5},{13,9},{1,13},{6,2},{10,6},{... | collective-permute-start | bytes 49160 | tf_op jit(solution)/shard_map/ppermute | solution.py:25
  89.8 5.8 %collective-permute-start.11 = (f32[1,16,136,4]{2,3,1,0:T(4,128)}, f32[1,16,136,4]{2,3,1,0:T(4,128)}, u32[]{:S(2)}, u32[]{:S(2)}) collective-permute-start(f32[1,16,136,4]{2,3,1,0:T(4,128)} %pad_maximum_fusion.22), channel_id=1, source_target_pairs={{1,0},{2,1},{3,2},{0,3},{5,4},{6,5},{7,6},{4,7},{9,8},{10,9},{11,1... | collective-permute-start | bytes 104456 | tf_op jit(solution)/shard_map/ppermute | solution.py:25
  93.6 5.7 %collective-permute-start.10 = (f32[1,16,136,4]{2,3,1,0:T(4,128)}, f32[1,16,136,4]{2,3,1,0:T(4,128)S(1)}, u32[]{:S(2)}, u32[]{:S(2)}) collective-permute-start(f32[1,16,136,4]{2,3,1,0:T(4,128)} %get-tuple-element.23), channel_id=1, source_target_pairs={{0,1},{1,2},{2,3},{3,0},{4,5},{5,6},{6,7},{7,4},{8,9},{9,10},{10,1... | collective-permute-start | bytes 104456 | tf_op jit(solution)/shard_map/ppermute | solution.py:23
  107.2 3.3 %collective-permute-start.13 = (f32[1,4,64,32]{2,3,1,0:T(8,128)S(1)}, f32[1,4,64,32]{2,3,1,0:T(8,128)S(1)}, u32[]{:S(2)}, u32[]{:S(2)}) collective-permute-start(f32[1,4,64,32]{2,3,1,0:T(8,128)S(1)} %slice.722), channel_id=1, source_target_pairs={{16,0},{32,16},{48,32},{64,48},{80,64},{96,80},{112,96},{0,112},{1... | collective-permute-start | bytes 98312 | tf_op jit(solution)/shard_map/ppermute | solution.py:25
  108.6 4.9 %collective-permute-start.12 = (f32[1,4,64,32]{2,3,1,0:T(8,128)S(1)}, f32[1,4,64,32]{2,3,1,0:T(8,128)S(1)}, u32[]{:S(2)}, u32[]{:S(2)}) collective-permute-start(f32[1,4,64,32]{2,3,1,0:T(8,128)S(1)} %slice.722), channel_id=1, source_target_pairs={{0,16},{16,32},{32,48},{48,64},{64,80},{80,96},{96,112},{112,0},{1... | collective-permute-start | bytes 98312 | tf_op jit(solution)/shard_map/ppermute | solution.py:23
  113.6 5.7 %collective-permute-start.14 = (f32[1,12,4,32]{2,3,1,0:T(8,128)S(1)}, f32[1,12,4,32]{2,3,1,0:T(8,128)S(1)}, u32[]{:S(2)}, u32[]{:S(2)}) collective-permute-start(f32[1,12,4,32]{2,3,1,0:T(8,128)S(1)} %get-tuple-element.47), channel_id=1, source_target_pairs={{0,4},{4,8},{8,12},{12,0},{1,5},{5,9},{9,13},{13,1},{2,6},{6,10},{... | collective-permute-start | bytes 18440 | tf_op jit(solution)/shard_map/ppermute | solution.py:23
  113.9 6.9 %collective-permute-start.15 = (f32[1,12,4,32]{2,3,1,0:T(8,128)S(1)}, f32[1,12,4,32]{2,3,1,0:T(8,128)S(1)}, u32[]{:S(2)}, u32[]{:S(2)}) collective-permute-start(f32[1,12,4,32]{2,3,1,0:T(8,128)S(1)} %get-tuple-element.48), channel_id=1, source_target_pairs={{4,0},{8,4},{12,8},{0,12},{5,1},{9,5},{13,9},{1,13},{6,2},{10,6},{... | collective-permute-start | bytes 18440 | tf_op jit(solution)/shard_map/ppermute | solution.py:25
  120.8 3.9 %collective-permute-start.17 = (f32[1,12,72,4]{2,3,1,0:T(4,128)S(1)}, f32[1,12,72,4]{2,3,1,0:T(4,128)S(1)}, u32[]{:S(2)}, u32[]{:S(2)}) collective-permute-start(f32[1,12,72,4]{2,3,1,0:T(4,128)S(1)} %pad_maximum_fusion.29), channel_id=1, source_target_pairs={{1,0},{2,1},{3,2},{0,3},{5,4},{6,5},{7,6},{4,7},{9,8},{10,9},{11,1... | collective-permute-start | bytes 41480 | tf_op jit(solution)/shard_map/ppermute | solution.py:25
  121.1 5.1 %collective-permute-start.16 = (f32[1,12,72,4]{2,3,1,0:T(4,128)S(1)}, f32[1,12,72,4]{2,3,1,0:T(4,128)S(1)}, u32[]{:S(2)}, u32[]{:S(2)}) collective-permute-start(f32[1,12,72,4]{2,3,1,0:T(4,128)S(1)} %get-tuple-element.30), channel_id=1, source_target_pairs={{0,1},{1,2},{2,3},{3,0},{4,5},{5,6},{6,7},{7,4},{8,9},{9,10},{10,1... | collective-permute-start | bytes 41480 | tf_op jit(solution)/shard_map/ppermute | solution.py:23
where the time goes:
time: 130 us; the launch traced here: 129 us
  waiting for transfers between devices  43.9 us (34%)
  local copies, waits for them, and re-layouts  33.9 us (26%)
  other arithmetic  28.2 us (22%)
  starting transfers between devices  22.1 us (17%)
    ppermute x9, waiting for transfers between devices, extended(): lax.ppermute(tail, axis, [(i, (i + 1) % count) for i in range(count)])  36 us
    ppermute x9, starting transfers between devices, extended(): lax.ppermute(head, axis, [((i + 1) % count, i) for i in range(count)])  16.7 us
    concatenate x3, other arithmetic, mirror_rims(): return jnp.concatenate([head_rows, core_rows, tail_rows], axis=axis_dim)  8.71 us
    ppermute x9, waiting for transfers between devices, extended(): lax.ppermute(head, axis, [((i + 1) % count, i) for i in range(count)])  7.95 us
    ppermute x9, starting transfers between devices, extended(): lax.ppermute(tail, axis, [(i, (i + 1) % count) for i in range(count)])  5.44 us
    another operation x6, local copies, waits for them, and re-layouts, stack_bands(): jnp.stack([lowpass, highpass], axis=1)  4.65 us
    slice x6, local copies, waits for them, and re-layouts, extended(): lax.slice_in_dim(cells, cells.shape[dim] - width, cells.shape[dim], axis=...  4.59 us
    another operation x14, other arithmetic, stack_bands(): jnp.stack([lowpass, highpass], axis=1)  4.44 us
  transfers between devices with their start and end apart: 18, of which 14 were waited for; matrix products, arithmetic and copies ran while one was open for 11% of the time, Pallas kernels for 0%

commit v1 on v0

v1 whole, which is shorter than its diff:
```python
import math

import jax
import jax.numpy as jnp
import numpy as np
from jax import lax
from jax.experimental import pallas as pl
from jax.experimental.pallas import tpu as pltpu
from jax.sharding import PartitionSpec as P

ALPHA = -1.586134342059924
BETA = -0.052980118572961
GAMMA = 0.882911075530934
DELTA = 0.443506852043971
SCALE_LOW = math.sqrt(2.0) / 1.230174104914001
SCALE_HIGH = 1.230174104914001 / math.sqrt(2.0)


def lift_matrix(rows, edges):
    s, d = rows[0::2], rows[1::2]
    none = np.zeros_like(s[:1])
    if edges == "periodic":
        d = d + ALPHA * (s + np.roll(s, -1, 0))
        s = s + BETA * (np.roll(d, 1, 0) + d)
        d = d + GAMMA * (s + np.roll(s, -1, 0))
        s = s + DELTA * (np.roll(d, 1, 0) + d)
        return s, d
    start, end = edges
    up = lambda v, last: np.concatenate([v[1:], last])
    down = lambda v, first: np.concatenate([first, v[:-1]])
    d1 = d + ALPHA * (s + up(s, s[-1:] if end else none))
    before1 = d1[:1] if start else ALPHA * s[:1]
    s1 = s + BETA * (down(d1, before1) + d1)
    d2 = d1 + GAMMA * (s1 + up(s1, s1[-1:] if end else BETA * d1[-1:]))
    before2 = d2[:1] if start else before1 + GAMMA * (BETA * before1 + s1[:1])
    return s1 + DELTA * (down(d2, before2) + d2), d2


def path_matrix(rows, level, edges):
    for _ in range(level):
        rows, high = lift_matrix(rows, edges)
    return np.concatenate([rows, high])


def outgoing(n):
    rows, left, right = np.eye(n), [], []
    for _ in range(3):
        s, d = rows[0::2], rows[1::2]
        left += [s[0], s[0] + BETA * (d[0] + ALPHA * (s[0] + s[1]))]
        right += [d[-1] + ALPHA * s[-1], s[-1] + BETA * (d[-2] + ALPHA * (s[-2] + s[-1]))]
        rows = lift_matrix(rows, (False, False))[0]
    return np.stack(left), np.stack(right)


def line_blocks(n, level):
    m = n >> level
    rows = np.eye(5 * n)
    for _ in range(level):
        rows, high = lift_matrix(rows, "periodic")
    whole = np.concatenate([rows[2 * m : 3 * m], high[2 * m : 3 * m]])
    return [whole[:, k * n : (k + 1) * n] for k in range(5)]


def solved(target, basis):
    u = np.linalg.lstsq(basis.T, target.T, rcond=None)[0].T
    assert np.abs(u @ basis - target).max() < 1e-9
    return np.where(np.abs(u) < 1e-10, 0.0, u)


def block_plan(n, level):
    left, right = outgoing(n)
    left, right = left[: 2 * level], right[: 2 * level]
    blocks = line_blocks(n, level)
    alone = path_matrix(np.eye(n), level, (False, False))
    from_left = solved(blocks[1], right)
    from_right = solved(blocks[3], left)
    own = solved(blocks[2] - alone, np.concatenate([left, right]))
    return dict(left=left, right=right, alone=alone, from_left=from_left, from_right=from_right, own_left=own[:, : 2 * level], own_right=own[:, 2 * level :])


def mirror_plan(n, level, plan):
    out = []
    m = n >> level
    for start in (True, False):
        rows = np.eye(4 * n)
        for _ in range(level):
            rows, high = lift_matrix(rows, (True, True))
        at = 0 if start else 3
        whole = np.concatenate([rows[at * m : (at + 1) * m], high[at * m : (at + 1) * m]])
        whole = whole[:, at * n : (at + 1) * n]
        rest = whole - plan["alone"] - plan["own_left"] @ plan["left"] - plan["own_right"] @ plan["right"]
        u = plan["from_left"] if start else plan["from_right"]
        g = np.linalg.lstsq(u, rest, rcond=None)[0]
        assert np.abs(u @ g - rest).max() < 1e-9
        out.append(np.where(np.abs(g) < 1e-10, 0.0, g))
    return out


MESH = pl.DeviceIdType.MESH
SIZES = {"gx": 8, "gy": 4, "gz": 4}
NX, NY, NZ = 16, 256, 128
F32 = jnp.float32


def rounded(matrix):
    return [[float(np.float32(c)) if abs(c) > 1e-10 else 0.0 for c in row] for row in matrix]


def fir(weights, rows):
    total = None
    for weight, row in zip(weights, rows):
        if weight == 0.0:
            continue
        term = row() if callable(row) else row
        term = term if weight == 1.0 else weight * term
        total = term if total is None else total + term
    return total


def lift_list(s, d, up, down, first, last):
    before1 = ALPHA * first(s)
    d1 = [b + ALPHA * (a + c) for a, b, c in zip(s, d, up(s, None))]
    s1 = [a + BETA * (b + c) for a, b, c in zip(s, d1, down(d1, before1))]
    d2 = [b + GAMMA * (a + c) for a, b, c in zip(s1, d1, up(s1, BETA * last(d1)))]
    before2 = before1 + GAMMA * (BETA * before1 + first(s1))
    s2 = [a + DELTA * (b + c) for a, b, c in zip(s1, d2, down(d2, before2))]
    return s2, d2


def lift_rows(src, base, n, dst, to, keep_high=True):
    k = n // 16
    s = [src[pl.ds(base + 16 * i, 8, stride=2), :] for i in range(k)]
    d = [src[pl.ds(base + 16 * i + 1, 8, stride=2), :] for i in range(k)]
    sub = lax.broadcasted_iota(jnp.int32, (8, 128), 0)
    top, bottom = sub == 0, sub == 7

    def up(v, fill):
        r = [pltpu.roll(x, 7, 0) for x in v]
        fill = jnp.zeros((8, 128), F32) if fill is None else fill
        return [jnp.where(bottom, r[i + 1] if i + 1 < k else fill, r[i]) for i in range(k)]

    def down(v, fill):
        r = [pltpu.roll(x, 1, 0) for x in v]
        return [jnp.where(top, r[i - 1] if i else fill, r[i]) for i in range(k)]

    low, high = lift_list(s, d, up, down, lambda v: v[0], lambda v: v[-1])
    for i in range(k):
        dst[pl.ds(to + 8 * i, 8), :] = low[i]
        if keep_high:
            dst[pl.ds(to + 8 * (k + i), 8), :] = high[i]


def lift_major(rows):
    low, high = lift_list(
        rows[0::2],
        rows[1::2],
        lambda v, fill: v[1:] + [jnp.zeros_like(v[0]) if fill is None else fill],
        lambda v, fill: [fill] + v[:-1],
        lambda v: v[0],
        lambda v: v[-1],
    )
    return low + high


class Side:
    def __init__(self, plan):
        self.groups = {}
        for source in ("from_left", "from_right", "own_left", "own_right"):
            u = plan[source]
            for g in range(u.shape[0] // 8):
                for f in range(u.shape[1]):
                    column = u[8 * g : 8 * g + 8, f]
                    if np.abs(column).max() > 1e-10:
                        self.groups.setdefault(g, []).append((source, f, column))


PLANS = {n: [block_plan(n, level) for level in (1, 2, 3)] for n in (NY, NZ)}
SIDES = {n: [Side(plan) for plan in PLANS[n]] for n in (NY, NZ)}
MIRRORS = [mirror_plan(NZ, level, PLANS[NZ][level - 1]) for level in (1, 2, 3)]
SEND_LEFT = {n: rounded(PLANS[n][2]["left"]) for n in (NY, NZ)}
SEND_RIGHT = {n: rounded(PLANS[n][2]["right"]) for n in (NY, NZ)}
SCALES = [(SCALE_LOW**level, SCALE_LOW ** (level - 1) * SCALE_HIGH) for level in (1, 2, 3)]


def factored(matrix):
    u, size, v = np.linalg.svd(matrix, full_matrices=False)
    rank = int((size > 1e-9).sum())
    return rounded(u[:, :rank] * size[:rank]), rounded(v[:rank])


X_ONE = block_plan(NX, 1)
X_ONE_LEFT, X_ONE_RIGHT = rounded(X_ONE["left"]), rounded(X_ONE["right"])
X_ONE_FROM_LEFT, X_ONE_FROM_RIGHT = rounded(X_ONE["from_left"]), rounded(X_ONE["from_right"])
X_TWO_BLOCKS = line_blocks(NX, 2)
X_TWO_FROM_LEFT, X_TWO_RIGHT = factored(X_TWO_BLOCKS[1])
X_TWO_FROM_RIGHT, X_TWO_LEFT = factored(X_TWO_BLOCKS[3])
X_TWO_OWN = rounded(X_TWO_BLOCKS[2])
X_THREE = [rounded(block) for block in line_blocks(NX, 3)]
N_TWO = len(X_TWO_RIGHT)

Y_ROWS = 6 * NX
Z_TWO, Z_THREE, Z_ROWS = 4 * NX, 8 * NX, 8 * NX + 6 * (NX // 2)
X23_ROWS = N_TWO * 64 + 64


def neighbour(axis, step):
    size = SIZES[axis]
    place = {name: lax.axis_index(name) for name in SIZES}
    place[axis] = lax.rem(place[axis] + (step + size), size)
    return tuple(place[name] for name in ("gx", "gy", "gz"))


def build_table(table, sides):
    sub = lax.broadcasted_iota(jnp.int32, (8, 128), 0)
    found = []
    at = 0
    for side in sides:
        places = {}
        for g, terms in side.groups.items():
            for source, f, column in terms:
                value = jnp.zeros((8, 128), F32)
                for i in range(8):
                    if abs(column[i]) > 1e-10:
                        value = jnp.where(sub == i, float(np.float32(column[i])), value)
                table[pl.ds(at, 8), :] = value
                places[g, source, f] = at
                at += 8
        found.append(places)
    return found


def table_rows(sides):
    return 8 * sum(len(terms) for side in sides for terms in side.groups.values())


def correct(ref, base, side, places, table, rows_of):
    for g, terms in side.groups.items():
        value = ref[pl.ds(base + 8 * g, 8), :]
        for source, f, _ in terms:
            value = value + table[pl.ds(places[g, source, f], 8), :] * rows_of(source, f)
        ref[pl.ds(base + 8 * g, 8), :] = value


def kernel(
    vel, out1, out2, out3, out4,
    v, y1, y2, y3, z1, z2, z3, w1, w2, w3, t2, t3, t4, ytab, ztab,
    ysl, ysr, yrl, yrr, zsl, zsr, zrl, zrr, zml, zmr,
    x1sl, x1sr, x1rl, x1rr, x23sl, x23sr, x23rl, x23rr, x3sl, x3sr, x3rl, x3rr,
    load_sem, send_sems, recv_sems,
):
    load = pltpu.make_async_copy(vel, v, load_sem)
    load.start()
    near = {
        "yl": neighbour("gy", -1), "yr": neighbour("gy", 1), "zl": neighbour("gz", -1), "zr": neighbour("gz", 1),
        "xl": neighbour("gx", -1), "xr": neighbour("gx", 1), "xll": neighbour("gx", -2), "xrr": neighbour("gx", 2),
    }
    barrier = pltpu.get_barrier_semaphore()
    for device in near.values():
        pl.semaphore_signal(barrier, inc=1, device_id=device, device_id_type=MESH)
    y_places = build_table(ytab, SIDES[NY])
    z_places = build_table(ztab, SIDES[NZ])

    def remote(index, src, dst, to):
        return pltpu.make_async_remote_copy(
            src_ref=src,
            dst_ref=dst,
            send_sem=send_sems.at[index],
            recv_sem=recv_sems.at[index],
            device_id=near[to],
            device_id_type=MESH,
        )

    load.wait()

    for h in range(2):
        head = [v[pl.ds(h * 8 * NY + k, 8, stride=NY), :] for k in range(21)]
        tail = [v[pl.ds(h * 8 * NY + k, 8, stride=NY), :] for k in range(NY - 28, NY)]
        for f in range(6):
            ysl[pl.ds(f * NX + 8 * h, 8), :] = fir(SEND_LEFT[NY][f][:21], head)
            ysr[pl.ds(f * NX + 8 * h, 8), :] = fir(SEND_RIGHT[NY][f][-28:], tail)
    pl.semaphore_wait(barrier, len(near))
    y_left = remote(0, ysl, yrr, "yl")
    y_right = remote(1, ysr, yrl, "yr")
    y_left.start()
    y_right.start()

    def lift_y(x, c):
        lift_rows(v, x * NY, NY, y1, x * NY)
        lift_rows(y1, x * NY, NY // 2, y2, x * (NY // 2))
        lift_rows(y2, x * (NY // 2), NY // 4, y3, x * (NY // 4))
        return c

    lax.fori_loop(0, NX, lift_y, 0)
    y_left.wait()
    y_right.wait()

    def finish_y(x, c):
        def rows_of(source, f):
            ref = {"from_left": yrl, "from_right": yrr, "own_left": ysl, "own_right": ysr}[source]
            return ref[pl.ds(f * NX + x, 1), :]

        for level, ref in enumerate((y1, y2, y3)):
            correct(ref, x * (NY >> level), SIDES[NY][level], y_places[level], ytab, rows_of)
        for t in range(2):
            z1[pl.ds(x * 256 + 128 * t, 128), :] = y1[pl.ds(x * NY + 128 * t, 128), :].T
        z2[pl.ds(x * 128, 128), :] = y2[pl.ds(x * 128, 128), :].T
        return c

    lax.fori_loop(0, NX, finish_y, 0)

    def turn_three(p, c):
        z3[pl.ds(p * 128, 128), :] = y3[pl.ds(p * 128, 128), :].T
        return c

    lax.fori_loop(0, NX // 2, turn_three, 0)

    def z_sums(level, load_row, store):
        left, right = SEND_LEFT[NZ][: 2 * level], SEND_RIGHT[NZ][: 2 * level]
        start, end = (rounded(m) for m in MIRRORS[level - 1])
        rows = {}

        def row(k):
            if k not in rows:
                rows[k] = load_row(k)
            return rows[k]

        for f in range(2 * level):
            for ref, weights in ((zsl, left), (zsr, right), (zml, start), (zmr, end)):
                ks = [k for k in range(NZ) if weights[f][k] != 0.0]
                store(ref, f, fir([weights[f][k] for k in ks], [row(k) for k in ks]))

    for h in range(2):
        for t in range(2):

            def store_one(ref, f, value, h=h, t=t):
                ref[pl.ds((f * 2 + t) * NX + 8 * h, 8), :] = value

            z_sums(1, lambda k, h=h, t=t: z1[pl.ds(h * 8 * 256 + t * 128 + k, 8, stride=256), :], store_one)

        def store_two(ref, f, value, h=h):
            ref[pl.ds(Z_TWO + f * NX + 8 * h, 8), :] = value

        z_sums(2, lambda k, h=h: z2[pl.ds(h * 8 * 128 + k, 8, stride=128), :], store_two)

    def store_three(ref, f, value):
        ref[pl.ds(Z_THREE + f * (NX // 2), 8), :] = value

    z_sums(3, lambda k: z3[pl.ds(k, 8, stride=128), :], store_three)
    z_left = remote(2, zsl, zrr, "zl")
    z_right = remote(3, zsr, zrl, "zr")
    z_left.start()
    z_right.start()

    def lift_z1(i, c):
        lift_rows(z1, i * NZ, NZ, w1, i * NZ)
        return c

    def lift_z2(x, c):
        lift_rows(z2, x * NZ, NZ, t2, x * 64, keep_high=False)
        lift_rows(t2, x * 64, 64, w2, x * 64)
        return c

    def lift_z3(p, c):
        lift_rows(z3, p * NZ, NZ, t3, p * 64, keep_high=False)
        lift_rows(t3, p * 64, 64, t4, p * 32, keep_high=False)
        lift_rows(t4, p * 32, 32, w3, p * 32)
        return c

    lax.fori_loop(0, 2 * NX, lift_z1, 0)
    lax.fori_loop(0, NX, lift_z2, 0)
    lax.fori_loop(0, NX // 2, lift_z3, 0)
    z_left.wait()
    z_right.wait()
    gz = lax.axis_index("gz")

    @pl.when(gz == 0)
    def _():
        zrl[...] = zml[...]

    @pl.when(gz == SIZES["gz"] - 1)
    def _():
        zrr[...] = zmr[...]

    z_refs = {"from_left": zrl, "from_right": zrr, "own_left": zsl, "own_right": zsr}

    def finish_z2(x, c):
        correct(w2, x * 64, SIDES[NZ][1], z_places[1], ztab, lambda s, f: z_refs[s][pl.ds(Z_TWO + f * NX + x, 1), :])
        return c

    def finish_z3(p, c):
        correct(w3, p * 32, SIDES[NZ][2], z_places[2], ztab, lambda s, f: z_refs[s][pl.ds(Z_THREE + f * 8 + p, 1), :])
        return c

    def finish_z1(x, c):
        for t in range(2):
            correct(
                w1, x * 256 + 128 * t, SIDES[NZ][0], z_places[0], ztab,
                lambda s, f, t=t: z_refs[s][pl.ds((f * 2 + t) * NX + x, 1), :],
            )
        return c

    lax.fori_loop(0, NX, finish_z2, 0)
    lax.fori_loop(0, NX // 2, finish_z3, 0)

    lane = lax.broadcasted_iota(jnp.int32, (8, 128), 1)
    low_lanes = lane < 64

    def sums_two(g, c):
        rows = [w2[pl.ds(x * 64 + 8 * g, 8), :] for x in range(NX)]
        for f in range(N_TWO):
            x23sl[pl.ds(f * 64 + 8 * g, 8), :] = fir(X_TWO_LEFT[f], rows)
            x23sr[pl.ds(f * 64 + 8 * g, 8), :] = fir(X_TWO_RIGHT[f], rows)
        return c

    def paired(weights, rows):
        total = jnp.zeros((8, 128), F32)
        for p in range(NX // 2):
            if weights[2 * p] == 0.0 and weights[2 * p + 1] == 0.0:
                continue
            total = total + jnp.where(low_lanes, weights[2 * p], weights[2 * p + 1]) * rows[p]
        return total + pltpu.roll(total, 64, 1)

    def sums_three(matrix, rows):
        return [
            jnp.where(low_lanes, paired(matrix[2 * h], rows), paired(matrix[2 * h + 1], rows)) for h in range(2)
        ]

    def send_three(g, c):
        rows = [w3[pl.ds(p * 32 + 8 * g, 8), :] for p in range(NX // 2)]
        for ref, block, at in ((x23sr, 1, N_TWO * 64), (x23sl, 3, N_TWO * 64), (x3sr, 0, 0), (x3sl, 4, 0)):
            for h, value in enumerate(sums_three(X_THREE[block], rows)):
                ref[pl.ds(at + 32 * h + 8 * g, 8), :] = value
        return c

    lax.fori_loop(0, 8, sums_two, 0)
    lax.fori_loop(0, 4, send_three, 0)
    x23_left = remote(4, x23sl, x23rr, "xl")
    x23_right = remote(5, x23sr, x23rl, "xr")
    x3_left = remote(6, x3sl, x3rr, "xll")
    x3_right = remote(7, x3sr, x3rl, "xrr")
    for copy in (x23_left, x23_right, x3_left, x3_right):
        copy.start()
    lax.fori_loop(0, NX, finish_z1, 0)

    def sums_one(g, c):
        rows = [w1[pl.ds(x * 256 + 8 * g, 8), :] for x in range(NX)]
        for f in range(2):
            x1sl[pl.ds(f * 256 + 8 * g, 8), :] = fir(X_ONE_LEFT[f], rows)
            x1sr[pl.ds(f * 256 + 8 * g, 8), :] = fir(X_ONE_RIGHT[f], rows)
        return c

    lax.fori_loop(0, 32, sums_one, 0)
    x1_left = remote(8, x1sl, x1rr, "xl")
    x1_right = remote(9, x1sr, x1rl, "xr")
    x1_left.start()
    x1_right.start()

    for copy in (x23_left, x23_right, x3_left, x3_right):
        copy.wait()

    def out_three(g, hz):
        rows = [w3[pl.ds(p * 32 + 8 * g, 8), :] for p in range(NX // 2)]
        own = sums_three(X_THREE[2], rows)
        high_y = (lane % 64) >= 32
        for hx in range(2):
            value = own[hx]
            for ref, at in ((x23rl, N_TWO * 64), (x23rr, N_TWO * 64), (x3rl, 0), (x3rr, 0)):
                value = value + ref[pl.ds(at + 32 * hx + 8 * g, 8), :]
            scale = SCALES[2][hx] * SCALES[2][hz]
            value = value * jnp.where(high_y, scale * SCALES[2][1], scale * SCALES[2][0])
            for q in range(4):
                i, hy = divmod(q, 2)
                band = 4 * hx + 2 * hy + hz
                row = 16 * i + 8 * (g % 2)
                piece = value[:, 32 * q : 32 * q + 32]
                if band:
                    out3[pl.ds((band - 1) * 32 + row, 8), :] = piece
                else:
                    out4[pl.ds(row, 8), :] = piece

    for g in range(4):
        out_three(g, g // 2)

    def out_two(g, hz):
        rows = [w2[pl.ds(x * 64 + 8 * g, 8), :] for x in range(NX)]
        left = [x23rl[pl.ds(f * 64 + 8 * g, 8), :] for f in range(N_TWO)]
        right = [x23rr[pl.ds(f * 64 + 8 * g, 8), :] for f in range(N_TWO)]
        for i in range(8):
            hx = i // 4
            value = fir(X_TWO_OWN[i] + X_TWO_FROM_LEFT[i] + X_TWO_FROM_RIGHT[i], rows + left + right)
            scale = SCALES[1][hx] * SCALES[1][hz]
            value = value * jnp.where(low_lanes, scale * SCALES[1][0], scale * SCALES[1][1])
            for hy in range(2):
                band = 4 * hx + 2 * hy + hz
                if band:
                    at = (band - 1) * 128 + (i % 4) * 32 + 8 * (g % 4)
                    out2[pl.ds(at, 8), :] = value[:, 64 * hy : 64 * hy + 64]

    for g in range(8):
        out_two(g, g // 4)

    x1_left.wait()
    x1_right.wait()

    for hy in range(2):
        for hz in range(2):

            def out_one(g, c, hy=hy, hz=hz):
                row = 128 * hy + 64 * hz + 8 * g
                rows = [w1[pl.ds(x * 256 + row, 8), :] for x in range(NX)]
                left = [x1rl[pl.ds(f * 256 + row, 8), :] for f in range(2)]
                right = [x1rr[pl.ds(f * 256 + row, 8), :] for f in range(2)]
                for i, value in enumerate(lift_major(rows)):
                    hx = i // 8
                    band = 4 * hx + 2 * hy + hz
                    if not band:
                        continue
                    value = fir([1.0] + X_ONE_FROM_LEFT[i] + X_ONE_FROM_RIGHT[i], [value] + left + right)
                    value = value * (SCALES[0][hx] * SCALES[0][hy] * SCALES[0][hz])
                    out1[pl.ds((band - 1) * 512 + (i % 8) * 64 + 8 * g, 8), :] = value
                return c

            lax.fori_loop(0, 8, out_one, 0)


def rows_of_scratch():
    rows = [16 * NY, 16 * NY, 16 * NY // 2, 16 * NY // 4]
    rows += [32 * NZ, 16 * NZ, 8 * NZ]
    rows += [32 * NZ, 16 * 64, 8 * 32]
    rows += [16 * 64, 8 * 64, 8 * 32]
    rows += [table_rows(SIDES[NY]), table_rows(SIDES[NZ])]
    rows += [Y_ROWS] * 4 + [Z_ROWS] * 6 + [512] * 4 + [X23_ROWS] * 4 + [64] * 4
    return rows


def shards(velocity):
    shapes = [(7 * 8 * 64, 128), (7 * 4 * 32, 64), (7 * 2 * 16, 32), (2 * 16, 32)]
    out1, out2, out3, out4 = pl.pallas_call(
        kernel,
        out_shape=[jax.ShapeDtypeStruct(shape, F32) for shape in shapes],
        in_specs=[pl.BlockSpec(memory_space=pl.ANY)],
        out_specs=[pl.BlockSpec(memory_space=pltpu.VMEM)] * 4,
        scratch_shapes=[pltpu.VMEM((rows, 128), F32) for rows in rows_of_scratch()]
        + [pltpu.SemaphoreType.DMA, pltpu.SemaphoreType.DMA((10,)), pltpu.SemaphoreType.DMA((10,))],
        compiler_params=pltpu.CompilerParams(collective_id=0, has_side_effects=True, vmem_limit_bytes=40 * 2**20),
    )(velocity.reshape(NX * NY, NZ))
    return (
        out1.reshape(7, 8, 64, 128).transpose(0, 1, 3, 2),
        out2.reshape(7, 4, 32, 64).transpose(0, 1, 3, 2),
        out3.reshape(7, 2, 16, 32).transpose(0, 1, 3, 2),
        out4.reshape(2, 16, 32).transpose(0, 2, 1),
    )


def solution(mesh):
    return jax.shard_map(
        shards,
        mesh=mesh,
        in_specs=(P("gx", "gy", "gz"),),
        out_specs=(
            P(None, "gx", "gy", "gz"),
            P(None, "gx", "gy", "gz"),
            P(None, "gx", "gy", "gz"),
            P("gx", "gy", "gz"),
        ),
        check_vma=False,
    )
```

time: 130 us -> 33 us (0.25)
  the two profiles are of different devices: /device:TPU:6 before, /device:TPU:1 now
where the time goes in v1:
time: 33 us; the launch traced here: 32.8 us
  Pallas kernels  27.4 us (83%)
  local copies, waits for them, and re-layouts  4.83 us (15%)
  between operations  0.65 us (2%)
    pallas_call x1, Pallas kernels, shards(): pl.pallas_call(kernel, out_shape=[jax.ShapeDtypeStruct(shape, F32) for sh...  27.4 us
    unnamed x6, local copies, waits for them, and re-layouts  4.83 us

profile of v1, /device:TPU:1, one launch (start us, length us, event | category | flops | bytes accessed | tf_op | source)
XLA Modules:
  0.0 32.8 jit_solution(15117012292025471687)
XLA Ops:
  0.6 0.0 copy-start
  0.6 1.6 %copy-done = f32[16,256,128]{2,1,0:T(8,128)S(1)} copy-done((f32[16,256,128]{2,1,0:T(8,128)S(1)}, f32[16,256,128]{2,1,0:T(8,128)}, u32[]{:S(2)}) %copy-start) | copy-done | bytes 2097176
  2.2 27.4 %shard_map.46 = (f32[3584,128]{1,0:T(8,128)S(1)}, f32[896,64]{1,0:T(8,128)S(1)}, f32[224,32]{1,0:T(8,128)S(1)}, f32[32,32]{1,0:T(8,128)S(1)}) custom-call(f32[4096,128]{1,0:T(8,128)S(1)} %bitcast.13), custom_call_target="tpu_custom_call" | custom-call | tf_op jit(solution)/shard_map/pallas_call | solution.py:538
  29.6 1.2 %copy.9 = f32[7,8,128,64]{2,3,1,0:T(8,128)} copy(f32[7,8,128,64]{2,3,1,0:T(8,128)S(1)} %bitcast.14) | data formatting | bytes 3670016
  30.8 0.8 %copy.10 = f32[7,4,64,32]{2,3,1,0:T(8,128)} copy(f32[7,4,64,32]{2,3,1,0:T(8,128)S(1)} %bitcast.15) | data formatting | bytes 458752
  31.6 0.6 %copy.11 = f32[7,2,32,16]{2,3,1,0:T(8,128)} copy(f32[7,2,32,16]{2,3,1,0:T(8,128)S(1)} %bitcast.16) | data formatting | bytes 57344
  32.2 0.6 %copy.12 = f32[2,32,16]{1,2,0:T(8,128)} copy(f32[2,32,16]{1,2,0:T(8,128)S(1)} %bitcast.17) | data formatting | bytes 8192
Async XLA Ops:
  0.6 1.6 %copy-start = (f32[16,256,128]{2,1,0:T(8,128)S(1)}, f32[16,256,128]{2,1,0:T(8,128)}, u32[]{:S(2)}) copy-start(f32[16,256,128]{2,1,0:T(8,128)} %param.1) | copy-start | bytes 6291460

commit v2 on v1

--- a/solution.py
+++ b/solution.py
@@ -2,6 +2,7 @@
 
 import jax
 import jax.numpy as jnp
+import ml_dtypes
 import numpy as np
 from jax import lax
 from jax.experimental import pallas as pl
@@ -78,20 +79,24 @@
     return dict(left=left, right=right, alone=alone, from_left=from_left, from_right=from_right, own_left=own[:, : 2 * level], own_right=own[:, 2 * level :])
 
 
-def mirror_plan(n, level, plan):
+def mirror_plan(n, plans):
     out = []
-    m = n >> level
     for start in (True, False):
-        rows = np.eye(4 * n)
-        for _ in range(level):
-            rows, high = lift_matrix(rows, (True, True))
-        at = 0 if start else 3
-        whole = np.concatenate([rows[at * m : (at + 1) * m], high[at * m : (at + 1) * m]])
-        whole = whole[:, at * n : (at + 1) * n]
-        rest = whole - plan["alone"] - plan["own_left"] @ plan["left"] - plan["own_right"] @ plan["right"]
-        u = plan["from_left"] if start else plan["from_right"]
-        g = np.linalg.lstsq(u, rest, rcond=None)[0]
-        assert np.abs(u @ g - rest).max() < 1e-9
+        uses, rests = [], []
+        for level, plan in enumerate(plans, 1):
+            m = n >> level
+            rows = np.eye(4 * n)
+            for _ in range(level):
+                rows, high = lift_matrix(rows, (True, True))
+            at = 0 if start else 3
+            whole = np.concatenate([rows[at * m : (at + 1) * m], high[at * m : (at + 1) * m]])
+            whole = whole[:, at * n : (at + 1) * n]
+            rests.append(whole - plan["alone"] - plan["own_left"] @ plan["left"] - plan["own_right"] @ plan["right"])
+            u = plan["from_left"] if start else plan["from_right"]
+            uses.append(np.pad(u, ((0, 0), (0, 6 - u.shape[1]))))
+        use, rest = np.concatenate(uses), np.concatenate(rests)
+        g = np.linalg.lstsq(use, rest, rcond=None)[0]
+        assert np.abs(use @ g - rest).max() < 1e-9
         out.append(np.where(np.abs(g) < 1e-10, 0.0, g))
     return out
 
@@ -176,7 +181,7 @@
 
 PLANS = {n: [block_plan(n, level) for level in (1, 2, 3)] for n in (NY, NZ)}
 SIDES = {n: [Side(plan) for plan in PLANS[n]] for n in (NY, NZ)}
-MIRRORS = [mirror_plan(NZ, level, PLANS[NZ][level - 1]) for level in (1, 2, 3)]
+MIRRORS = mirror_plan(NZ, PLANS[NZ])
 SEND_LEFT = {n: rounded(PLANS[n][2]["left"]) for n in (NY, NZ)}
 SEND_RIGHT = {n: rounded(PLANS[n][2]["right"]) for n in (NY, NZ)}
 SCALES = [(SCALE_LOW**level, SCALE_LOW ** (level - 1) * SCALE_HIGH) for level in (1, 2, 3)]
@@ -233,23 +238,95 @@
     return 8 * sum(len(terms) for side in sides for terms in side.groups.values())
 
 
-def correct(ref, base, side, places, table, rows_of):
+def correct(ref, base, side, places, table, refs, row):
     for g, terms in side.groups.items():
+        terms = [(source, f) for source, f, _ in terms if source in refs]
+        if not terms:
+            continue
         value = ref[pl.ds(base + 8 * g, 8), :]
-        for source, f, _ in terms:
-            value = value + table[pl.ds(places[g, source, f], 8), :] * rows_of(source, f)
+        for source, f in terms:
+            value = value + table[pl.ds(places[g, source, f], 8), :] * refs[source][pl.ds(row(f), 1), :]
         ref[pl.ds(base + 8 * g, 8), :] = value
 
 
+def parts_of(value):
+    rest, parts = np.asarray(value, np.float32), []
+    for _ in range(3):
+        part = rest.astype(ml_dtypes.bfloat16)
+        parts.append(part)
+        rest = rest - part.astype(np.float32)
+    return parts
+
+
+def spread(level):
+    plan = PLANS[NY][level - 1]
+    left, right = plan["from_left"].T, plan["from_right"].T
+    if level == 3:
+        blocks = []
+        for u in (left, right):
+            block = np.zeros((8, NX, 128))
+            block[:6, 0::2, :64] = u[:, None, :]
+            block[:6, 1::2, 64:] = u[:, None, :]
+            blocks.append(block.reshape(128, 128))
+        matrix = np.concatenate(blocks)
+    else:
+        matrix = np.repeat(np.concatenate([left, right]), NX, axis=0)
+    one, two, three = parts_of(matrix)
+    return np.concatenate([one, two, three, one, two, one])
+
+
+SPREADS = [spread(level) for level in (1, 2, 3)]
+Z_SENDS = np.zeros((32, NZ), np.float32)
+for _at, _rows in enumerate((PLANS[NZ][2]["left"], PLANS[NZ][2]["right"], *MIRRORS)):
+    Z_SENDS[8 * _at : 8 * _at + 6] = _rows
+
+
+def split(value):
+    one = value.astype(jnp.bfloat16).astype(F32)
+    two = (value - one).astype(jnp.bfloat16).astype(F32)
+    return one, two, value - one - two
+
+
+def lanes_of(shape):
+    return lax.broadcasted_iota(jnp.int32, shape, 1)
+
+
+def slots(level, left, right):
+    lane = lanes_of(left.shape)
+    turn = lambda value, by: pltpu.roll(value, by, 1)
+    if level == 1:
+        one, two, three = split(jnp.where(lane < 32, left, jnp.where(lane < 64, turn(right, 32), 0.0)))
+        return [one + turn(one, 64), one + turn(two, 64), two + turn(three, 64)]
+    if level == 2:
+        one, two, three = split(jnp.where(lane < 64, left, turn(right, 64)))
+        return [one, one, one, two, two, three]
+    one, two, three = zip(split(left), split(right))
+    return [*one, *one, *one, *two, *two, *three]
+
+
+def expand(level, arrays, keep, spread_ref):
+    factor = jnp.concatenate([jnp.where(keep, a, 0.0).astype(jnp.bfloat16) for a in arrays], axis=1)
+    return jnp.dot(factor, spread_ref[...], preferred_element_type=F32)
+
+
 def kernel(
-    vel, out1, out2, out3, out4,
-    v, y1, y2, y3, z1, z2, z3, w1, w2, w3, t2, t3, t4, ytab, ztab,
+    vel, spread1_hbm, spread2_hbm, spread3_hbm, sends_hbm,
+    w1, w2, w3, x1rl, x1rr, x23rl, x23rr, x3rl, x3rr,
+    v, y1, y2, y3, z1, z2, z3, t2, t3, t4, ytab, ztab,
     ysl, ysr, yrl, yrr, zsl, zsr, zrl, zrr, zml, zmr,
-    x1sl, x1sr, x1rl, x1rr, x23sl, x23sr, x23rl, x23rr, x3sl, x3sr, x3rl, x3rr,
-    load_sem, send_sems, recv_sems,
+    htl, htr, g1, g2, g3, u2, u3, p1, p2, p3, zlsl, zlsr, zlrl, zlrr, zlml, zlmr,
+    x1sl, x1sr, x23sl, x23sr, x3sl, x3sr, xesl, xesr, xerl, xerr,
+    spread1, spread2, spread3, sends,
+    load_sems, send_sems, recv_sems,
 ):
-    load = pltpu.make_async_copy(vel, v, load_sem)
-    load.start()
+    loads = [
+        pltpu.make_async_copy(src, dst, load_sems.at[i])
+        for i, (src, dst) in enumerate(
+            ((vel, v), (sends_hbm, sends), (spread1_hbm, spread1), (spread2_hbm, spread2), (spread3_hbm, spread3))
+        )
+    ]
+    for load in loads:
+        load.start()
     near = {
         "yl": neighbour("gy", -1), "yr": neighbour("gy", 1), "zl": neighbour("gz", -1), "zr": neighbour("gz", 1),
         "xl": neighbour("gx", -1), "xr": neighbour("gx", 1), "xll": neighbour("gx", -2), "xrr": neighbour("gx", 2),
@@ -259,6 +336,8 @@
         pl.semaphore_signal(barrier, inc=1, device_id=device, device_id_type=MESH)
     y_places = build_table(ytab, SIDES[NY])
     z_places = build_table(ztab, SIDES[NZ])
+    for ref in (yrl, yrr):
+        ref[pl.ds(Y_ROWS, 32), :] = jnp.zeros((32, 128), F32)
 
     def remote(index, src, dst, to):
         return pltpu.make_async_remote_copy(
@@ -270,7 +349,7 @@
             device_id_type=MESH,
         )
 
-    load.wait()
+    loads[0].wait()
 
     for h in range(2):
         head = [v[pl.ds(h * 8 * NY + k, 8, stride=NY), :] for k in range(21)]
@@ -278,45 +357,37 @@
         for f in range(6):
             ysl[pl.ds(f * NX + 8 * h, 8), :] = fir(SEND_LEFT[NY][f][:21], head)
             ysr[pl.ds(f * NX + 8 * h, 8), :] = fir(SEND_RIGHT[NY][f][-28:], tail)
-    pl.semaphore_wait(barrier, len(near))
-    y_left = remote(0, ysl, yrr, "yl")
-    y_right = remote(1, ysr, yrl, "yr")
-    y_left.start()
-    y_right.start()
 
     def lift_y(x, c):
         lift_rows(v, x * NY, NY, y1, x * NY)
         lift_rows(y1, x * NY, NY // 2, y2, x * (NY // 2))
         lift_rows(y2, x * (NY // 2), NY // 4, y3, x * (NY // 4))
+        own = {"own_left": ysl, "own_right": ysr}
+        for level, ref in ((1, y2), (2, y3)):
+            correct(ref, x * (NY >> level), SIDES[NY][level], y_places[level], ytab, own, lambda f: f * NX + x)
         return c
 
     lax.fori_loop(0, NX, lift_y, 0)
-    y_left.wait()
-    y_right.wait()
-
-    def finish_y(x, c):
-        def rows_of(source, f):
-            ref = {"from_left": yrl, "from_right": yrr, "own_left": ysl, "own_right": ysr}[source]
-            return ref[pl.ds(f * NX + x, 1), :]
-
-        for level, ref in enumerate((y1, y2, y3)):
-            correct(ref, x * (NY >> level), SIDES[NY][level], y_places[level], ytab, rows_of)
+    pl.semaphore_wait(barrier, len(near))
+    y_left = remote(0, ysl, yrr.at[pl.ds(0, Y_ROWS)], "yl")
+    y_right = remote(1, ysr, yrl.at[pl.ds(0, Y_ROWS)], "yr")
+    y_left.start()
+    y_right.start()
+
+    def turn(x, c):
         for t in range(2):
             z1[pl.ds(x * 256 + 128 * t, 128), :] = y1[pl.ds(x * NY + 128 * t, 128), :].T
         z2[pl.ds(x * 128, 128), :] = y2[pl.ds(x * 128, 128), :].T
         return c
 
-    lax.fori_loop(0, NX, finish_y, 0)
-
     def turn_three(p, c):
         z3[pl.ds(p * 128, 128), :] = y3[pl.ds(p * 128, 128), :].T
         return c
 
-    lax.fori_loop(0, NX // 2, turn_three, 0)
+    lax.fori_loop(0, NX, turn, 0, unroll=2)
+    lax.fori_loop(0, NX // 2, turn_three, 0, unroll=2)
 
     def z_sums(level, load_row, store):
-        left, right = SEND_LEFT[NZ][: 2 * level], SEND_RIGHT[NZ][: 2 * level]
-        start, end = (rounded(m) for m in MIRRORS[level - 1])
         rows = {}
 
         def row(k):
@@ -325,9 +396,10 @@
             return rows[k]
 
         for f in range(2 * level):
-            for ref, weights in ((zsl, left), (zsr, right), (zml, start), (zmr, end)):
-                ks = [k for k in range(NZ) if weights[f][k] != 0.0]
-                store(ref, f, fir([weights[f][k] for k in ks], [row(k) for k in ks]))
+            for at, ref in enumerate((zsl, zsr, zml, zmr)):
+                weights = [float(c) for c in Z_SENDS[8 * at + f]]
+                ks = [k for k in range(NZ) if weights[k] != 0.0]
+                store(ref, f, fir([weights[k] for k in ks], [row(k) for k in ks]))
 
     for h in range(2):
         for t in range(2):
@@ -351,59 +423,166 @@
     z_left.start()
     z_right.start()
 
-    def lift_z1(i, c):
-        lift_rows(z1, i * NZ, NZ, w1, i * NZ)
-        return c
+    row_one = lambda x, t: lambda f: (f * 2 + t) * NX + x
+    row_two = lambda x: lambda f: Z_TWO + f * NX + x
+    row_three = lambda p: lambda f: Z_THREE + f * (NX // 2) + p
+    z_own = {"own_left": zsl, "own_right": zsr}
 
     def lift_z2(x, c):
         lift_rows(z2, x * NZ, NZ, t2, x * 64, keep_high=False)
         lift_rows(t2, x * 64, 64, w2, x * 64)
+        correct(w2, x * 64, SIDES[NZ][1], z_places[1], ztab, z_own, row_two(x))
         return c
 
     def lift_z3(p, c):
         lift_rows(z3, p * NZ, NZ, t3, p * 64, keep_high=False)
         lift_rows(t3, p * 64, 64, t4, p * 32, keep_high=False)
         lift_rows(t4, p * 32, 32, w3, p * 32)
-        return c
+        correct(w3, p * 32, SIDES[NZ][2], z_places[2], ztab, z_own, row_three(p))
+        return c
+
+    def lift_z1(i, c):
+        lift_rows(z1, i * NZ, NZ, w1, i * NZ)
+        return c
+
+    lax.fori_loop(0, NX // 2, lift_z3, 0)
+    lax.fori_loop(0, NX, lift_z2, 0)
+
+    y_left.wait()
+    y_right.wait()
+    for load in loads[1:]:
+        load.wait()
+    htl[...] = yrl[...].T
+    htr[...] = yrr[...].T
+    for at, ref in ((0, htl), (8, htr)):
+        sums = jnp.dot(sends[...], ref[...], precision=lax.Precision.HIGHEST, preferred_element_type=F32)
+        for i, out in enumerate((zlsl, zlsr, zlml, zlmr)):
+            out[pl.ds(at, 8), :] = sums[8 * i : 8 * i + 8]
+    zl_left = remote(4, zlsl, zlrr, "zl")
+    zl_right = remote(5, zlsr, zlrl, "zr")
+    zl_left.start()
+    zl_right.start()
+
+    for i, ref in enumerate((htl, htr)):
+        lift_rows(ref, 0, 128, g1, 128 * i)
+        lift_rows(g1, 128 * i, 64, u2, 64 * i)
+        lift_rows(u2, 64 * i, 32, u3, 32 * i)
+    for i in range(2):
+        own = {"own_left": zlsl, "own_right": zlsr}
+        g2[pl.ds(64 * i, 64), :] = u2[pl.ds(64 * i, 64), :]
+        g3[pl.ds(32 * i, 32), :] = u3[pl.ds(32 * i, 32), :]
+        correct(g2, 64 * i, SIDES[NZ][1], z_places[1], ztab, own, lambda f, i=i: 8 * i + f)
+        correct(g3, 32 * i, SIDES[NZ][2], z_places[2], ztab, own, lambda f, i=i: 8 * i + f)
+    for level, g, p, n in ((1, g1, p1, 128), (2, g2, p2, 64), (3, g3, p3, 32)):
+        for i, value in enumerate(slots(level, g[pl.ds(0, n), :], g[pl.ds(n, n), :])):
+            p[pl.ds(n * i, n), :] = value
 
     lax.fori_loop(0, 2 * NX, lift_z1, 0)
-    lax.fori_loop(0, NX, lift_z2, 0)
-    lax.fori_loop(0, NX // 2, lift_z3, 0)
-    z_left.wait()
-    z_right.wait()
+
+    def spread_one(x, c):
+        keep = (lanes_of((128, 128)) & 15) == x
+        value = expand(1, [p1[pl.ds(128 * i, 128), :] for i in range(3)], keep, spread1)
+        for t in range(2):
+            at = pl.ds(x * 256 + 128 * t, 128)
+            w1[at, :] = w1[at, :] + value[:, 128 * t : 128 * t + 128]
+        return c
+
+    def spread_two(x, c):
+        keep = (lanes_of((64, 128)) & 15) == x
+        at = pl.ds(x * 64, 64)
+        w2[at, :] = w2[at, :] + expand(2, [p2[pl.ds(64 * i, 64), :] for i in range(6)], keep, spread2)
+        return c
+
+    def spread_three(p, c):
+        keep = ((lanes_of((32, 128)) & 15) >> 1) == p
+        at = pl.ds(p * 32, 32)
+        w3[at, :] = w3[at, :] + expand(3, [p3[pl.ds(32 * i, 32), :] for i in range(12)], keep, spread3)
+        return c
+
+    lax.fori_loop(0, NX, spread_one, 0)
+
+    def sums_one(g, c):
+        rows = [w1[pl.ds(x * 256 + 8 * g, 8), :] for x in (0, 1, 2, 12, 13, 14, 15)]
+        for f in range(2):
+            x1sl[pl.ds(f * 256 + 8 * g, 8), :] = fir(X_ONE_LEFT[f][:3], rows[:3])
+            x1sr[pl.ds(f * 256 + 8 * g, 8), :] = fir(X_ONE_RIGHT[f][12:], rows[3:])
+        return c
+
+    lax.fori_loop(0, 32, sums_one, 0, unroll=4)
+    x1_left = remote(6, x1sl, x1rr, "xl")
+    x1_right = remote(7, x1sr, x1rl, "xr")
+    x1_left.start()
+    x1_right.start()
+    lax.fori_loop(0, NX // 2, spread_three, 0)
+    lax.fori_loop(0, NX, spread_two, 0)
+
+    for copy in (z_left, z_right, zl_left, zl_right):
+        copy.wait()
     gz = lax.axis_index("gz")
 
     @pl.when(gz == 0)
     def _():
         zrl[...] = zml[...]
+        zlrl[...] = zlml[...]
 
     @pl.when(gz == SIZES["gz"] - 1)
     def _():
         zrr[...] = zmr[...]
-
-    z_refs = {"from_left": zrl, "from_right": zrr, "own_left": zsl, "own_right": zsr}
+        zlrr[...] = zlmr[...]
+
+    lane, sub = lanes_of((16, 128)), lax.broadcasted_iota(jnp.int32, (16, 128), 0)
+    for late, ref in ((zlrl, zrl), (zlrr, zrr)):
+        left, right = late[pl.ds(0, 8), :], late[pl.ds(8, 8), :]
+        for level, spread_ref, count in ((3, spread3, 8), (2, spread2, NX), (1, spread1, NX)):
+            arrays = slots(level, left, right)
+            if level == 3:
+                keep = ((lane[:8] & 15) >> 1) == sub[:8]
+            else:
+                keep = (lane & 15) == sub
+            tall = [
+                jnp.concatenate([jnp.where(keep, a[f : f + 1], 0.0) for f in range(2 * level)], axis=0) for a in arrays
+            ]
+            value = expand(level, tall, jnp.full(tall[0].shape, True), spread_ref)
+            for f in range(2 * level):
+                piece = value[f * count : f * count + count]
+                if level == 1:
+                    for t in range(2):
+                        at = pl.ds((f * 2 + t) * NX, NX)
+                        ref[at, :] = ref[at, :] + piece[:, 128 * t : 128 * t + 128]
+                else:
+                    at = pl.ds((Z_TWO if level == 2 else Z_THREE) + f * count, count)
+                    ref[at, :] = ref[at, :] + piece
+
+    for side, ref in enumerate((zrl, zrr)):
+        for f in range(2):
+            for t in range(2):
+                rows = [ref[pl.ds((f * 2 + t) * NX + x, 1), :] for x in (0, 1, 2, 12, 13, 14, 15)]
+                for xf in range(2):
+                    at = pl.ds((xf * 2 + t) * 4 + side * 2 + f, 1)
+                    xesl[at, :] = fir(X_ONE_LEFT[xf][:3], rows[:3])
+                    xesr[at, :] = fir(X_ONE_RIGHT[xf][12:], rows[3:])
+    xe_left = remote(8, xesl, xerr, "xl")
+    xe_right = remote(9, xesr, xerl, "xr")
+    xe_left.start()
+    xe_right.start()
+
+    z_past = {"from_left": zrl, "from_right": zrr}
 
     def finish_z2(x, c):
-        correct(w2, x * 64, SIDES[NZ][1], z_places[1], ztab, lambda s, f: z_refs[s][pl.ds(Z_TWO + f * NX + x, 1), :])
+        correct(w2, x * 64, SIDES[NZ][1], z_places[1], ztab, z_past, row_two(x))
         return c
 
     def finish_z3(p, c):
-        correct(w3, p * 32, SIDES[NZ][2], z_places[2], ztab, lambda s, f: z_refs[s][pl.ds(Z_THREE + f * 8 + p, 1), :])
+        correct(w3, p * 32, SIDES[NZ][2], z_places[2], ztab, z_past, row_three(p))
         return c
 
     def finish_z1(x, c):
         for t in range(2):
-            correct(
-                w1, x * 256 + 128 * t, SIDES[NZ][0], z_places[0], ztab,
-                lambda s, f, t=t: z_refs[s][pl.ds((f * 2 + t) * NX + x, 1), :],
-            )
-        return c
-
+            correct(w1, x * 256 + 128 * t, SIDES[NZ][0], z_places[0], ztab, z_past, row_one(x, t))
+        return c
+
+    lax.fori_loop(0, NX // 2, finish_z3, 0)
     lax.fori_loop(0, NX, finish_z2, 0)
-    lax.fori_loop(0, NX // 2, finish_z3, 0)
-
-    lane = lax.broadcasted_iota(jnp.int32, (8, 128), 1)
-    low_lanes = lane < 64
 
     def sums_two(g, c):
         rows = [w2[pl.ds(x * 64 + 8 * g, 8), :] for x in range(NX)]
@@ -412,19 +591,6 @@
             x23sr[pl.ds(f * 64 + 8 * g, 8), :] = fir(X_TWO_RIGHT[f], rows)
         return c
 
-    def paired(weights, rows):
-        total = jnp.zeros((8, 128), F32)
-        for p in range(NX // 2):
-            if weights[2 * p] == 0.0 and weights[2 * p + 1] == 0.0:
-                continue
-            total = total + jnp.where(low_lanes, weights[2 * p], weights[2 * p + 1]) * rows[p]
-        return total + pltpu.roll(total, 64, 1)
-
-    def sums_three(matrix, rows):
-        return [
-            jnp.where(low_lanes, paired(matrix[2 * h], rows), paired(matrix[2 * h + 1], rows)) for h in range(2)
-        ]
-
     def send_three(g, c):
         rows = [w3[pl.ds(p * 32 + 8 * g, 8), :] for p in range(NX // 2)]
         for ref, block, at in ((x23sr, 1, N_TWO * 64), (x23sl, 3, N_TWO * 64), (x3sr, 0, 0), (x3sl, 4, 0)):
@@ -434,52 +600,74 @@
 
     lax.fori_loop(0, 8, sums_two, 0)
     lax.fori_loop(0, 4, send_three, 0)
-    x23_left = remote(4, x23sl, x23rr, "xl")
-    x23_right = remote(5, x23sr, x23rl, "xr")
-    x3_left = remote(6, x3sl, x3rr, "xll")
-    x3_right = remote(7, x3sr, x3rl, "xrr")
+    x23_left = remote(10, x23sl, x23rr, "xl")
+    x23_right = remote(11, x23sr, x23rl, "xr")
+    x3_left = remote(12, x3sl, x3rr, "xll")
+    x3_right = remote(13, x3sr, x3rl, "xrr")
     for copy in (x23_left, x23_right, x3_left, x3_right):
         copy.start()
     lax.fori_loop(0, NX, finish_z1, 0)
-
-    def sums_one(g, c):
-        rows = [w1[pl.ds(x * 256 + 8 * g, 8), :] for x in range(NX)]
-        for f in range(2):
-            x1sl[pl.ds(f * 256 + 8 * g, 8), :] = fir(X_ONE_LEFT[f], rows)
-            x1sr[pl.ds(f * 256 + 8 * g, 8), :] = fir(X_ONE_RIGHT[f], rows)
-        return c
-
-    lax.fori_loop(0, 32, sums_one, 0)
-    x1_left = remote(8, x1sl, x1rr, "xl")
-    x1_right = remote(9, x1sr, x1rl, "xr")
-    x1_left.start()
-    x1_right.start()
-
+    for copy in (x1_left, x1_right, xe_left, xe_right):
+        copy.wait()
+    for xf in range(2):
+        for t in range(2):
+            for ref, ends in ((x1rl, xerl), (x1rr, xerr)):
+                at = (xf * 2 + t) * 4
+                refs = {"from_left": ends.at[pl.ds(at, 2)], "from_right": ends.at[pl.ds(at + 2, 2)]}
+                correct(ref, xf * 256 + 128 * t, SIDES[NZ][0], z_places[0], ztab, refs, lambda f: f)
     for copy in (x23_left, x23_right, x3_left, x3_right):
         copy.wait()
 
-    def out_three(g, hz):
-        rows = [w3[pl.ds(p * 32 + 8 * g, 8), :] for p in range(NX // 2)]
-        own = sums_three(X_THREE[2], rows)
-        high_y = (lane % 64) >= 32
-        for hx in range(2):
-            value = own[hx]
-            for ref, at in ((x23rl, N_TWO * 64), (x23rr, N_TWO * 64), (x3rl, 0), (x3rr, 0)):
-                value = value + ref[pl.ds(at + 32 * hx + 8 * g, 8), :]
-            scale = SCALES[2][hx] * SCALES[2][hz]
-            value = value * jnp.where(high_y, scale * SCALES[2][1], scale * SCALES[2][0])
-            for q in range(4):
-                i, hy = divmod(q, 2)
+
+def paired(weights, rows):
+    low_lanes = lanes_of((8, 128)) < 64
+    total = jnp.zeros((8, 128), F32)
+    for p in range(NX // 2):
+        if weights[2 * p] == 0.0 and weights[2 * p + 1] == 0.0:
+            continue
+        total = total + jnp.where(low_lanes, weights[2 * p], weights[2 * p + 1]) * rows[p]
+    return total + pltpu.roll(total, 64, 1)
+
+
+def sums_three(matrix, rows):
+    low_lanes = lanes_of((8, 128)) < 64
+    return [jnp.where(low_lanes, paired(matrix[2 * h], rows), paired(matrix[2 * h + 1], rows)) for h in range(2)]
+
+
+def finish(w1, w2, w3, x1rl, x1rr, x23rl, x23rr, x3rl, x3rr, out1, out2, out3, out4, o1, o2, o3, o4, sems):
+    lane = lanes_of((8, 128))
+    low_lanes = lane < 64
+    copies = []
+
+    def send(src, dst):
+        copy = pltpu.make_async_copy(src, dst, sems.at[len(copies)])
+        copy.start()
+        copies.append(copy)
+
+    for hy in range(2):
+        for hz in range(2):
+
+            def out_one(g, c, hy=hy, hz=hz):
+                row = 128 * hy + 64 * hz + 8 * g
+                rows = [w1[pl.ds(x * 256 + row, 8), :] for x in range(NX)]
+                left = [x1rl[pl.ds(f * 256 + row, 8), :] for f in range(2)]
+                right = [x1rr[pl.ds(f * 256 + row, 8), :] for f in range(2)]
+                for i, value in enumerate(lift_major(rows)):
+                    hx = i // 8
+                    band = 4 * hx + 2 * hy + hz
+                    if not band:
+                        continue
+                    value = fir([1.0] + X_ONE_FROM_LEFT[i] + X_ONE_FROM_RIGHT[i], [value] + left + right)
+                    value = value * (SCALES[0][hx] * SCALES[0][hy] * SCALES[0][hz])
+                    o1[pl.ds((band - 1) * 512 + (i % 8) * 64 + 8 * g, 8), :] = value
+                return c
+
+            lax.fori_loop(0, 8, out_one, 0)
+            for hx in range(2):
                 band = 4 * hx + 2 * hy + hz
-                row = 16 * i + 8 * (g % 2)
-                piece = value[:, 32 * q : 32 * q + 32]
                 if band:
-                    out3[pl.ds((band - 1) * 32 + row, 8), :] = piece
-                else:
-                    out4[pl.ds(row, 8), :] = piece
-
-    for g in range(4):
-        out_three(g, g // 2)
+                    at = pl.ds((band - 1) * 512, 512)
+                    send(o1.at[at], out1.at[at])
 
     def out_two(g, hz):
         rows = [w2[pl.ds(x * 64 + 8 * g, 8), :] for x in range(NX)]
@@ -494,56 +682,72 @@
                 band = 4 * hx + 2 * hy + hz
                 if band:
                     at = (band - 1) * 128 + (i % 4) * 32 + 8 * (g % 4)
-                    out2[pl.ds(at, 8), :] = value[:, 64 * hy : 64 * hy + 64]
+                    o2[pl.ds(at, 8), :] = value[:, 64 * hy : 64 * hy + 64]
 
     for g in range(8):
         out_two(g, g // 4)
-
-    x1_left.wait()
-    x1_right.wait()
-
-    for hy in range(2):
-        for hz in range(2):
-
-            def out_one(g, c, hy=hy, hz=hz):
-                row = 128 * hy + 64 * hz + 8 * g
-                rows = [w1[pl.ds(x * 256 + row, 8), :] for x in range(NX)]
-                left = [x1rl[pl.ds(f * 256 + row, 8), :] for f in range(2)]
-                right = [x1rr[pl.ds(f * 256 + row, 8), :] for f in range(2)]
-                for i, value in enumerate(lift_major(rows)):
-                    hx = i // 8
-                    band = 4 * hx + 2 * hy + hz
-                    if not band:
-                        continue
-                    value = fir([1.0] + X_ONE_FROM_LEFT[i] + X_ONE_FROM_RIGHT[i], [value] + left + right)
-                    value = value * (SCALES[0][hx] * SCALES[0][hy] * SCALES[0][hz])
-                    out1[pl.ds((band - 1) * 512 + (i % 8) * 64 + 8 * g, 8), :] = value
-                return c
-
-            lax.fori_loop(0, 8, out_one, 0)
-
-
-def rows_of_scratch():
-    rows = [16 * NY, 16 * NY, 16 * NY // 2, 16 * NY // 4]
-    rows += [32 * NZ, 16 * NZ, 8 * NZ]
-    rows += [32 * NZ, 16 * 64, 8 * 32]
-    rows += [16 * 64, 8 * 64, 8 * 32]
-    rows += [table_rows(SIDES[NY]), table_rows(SIDES[NZ])]
-    rows += [Y_ROWS] * 4 + [Z_ROWS] * 6 + [512] * 4 + [X23_ROWS] * 4 + [64] * 4
-    return rows
+    send(o2, out2)
+
+    def out_three(g, hz):
+        rows = [w3[pl.ds(p * 32 + 8 * g, 8), :] for p in range(NX // 2)]
+        own = sums_three(X_THREE[2], rows)
+        high_y = (lane & 63) >= 32
+        for hx in range(2):
+            value = own[hx]
+            for ref, at in ((x23rl, N_TWO * 64), (x23rr, N_TWO * 64), (x3rl, 0), (x3rr, 0)):
+                value = value + ref[pl.ds(at + 32 * hx + 8 * g, 8), :]
+            scale = SCALES[2][hx] * SCALES[2][hz]
+            value = value * jnp.where(high_y, scale * SCALES[2][1], scale * SCALES[2][0])
+            for q in range(4):
+                i, hy = divmod(q, 2)
+                band = 4 * hx + 2 * hy + hz
+                row = 16 * i + 8 * (g % 2)
+                piece = value[:, 32 * q : 32 * q + 32]
+                if band:
+                    o3[pl.ds((band - 1) * 32 + row, 8), :] = piece
+                else:
+                    o4[pl.ds(row, 8), :] = piece
+
+    for g in range(4):
+        out_three(g, g // 2)
+    send(o3, out3)
+    send(o4, out4)
+    for copy in copies:
+        copy.wait()
 
 
 def shards(velocity):
+    vmem, hbm = pl.BlockSpec(memory_space=pltpu.VMEM), pl.BlockSpec(memory_space=pltpu.HBM)
+    wide = lambda rows: pltpu.VMEM((rows, 128), F32)
+    results = [32 * NZ, 16 * 64, 8 * 32, 512, 512, X23_ROWS, X23_ROWS, 64, 64]
+    scratch = [16 * NY, 16 * NY, 16 * NY // 2, 16 * NY // 4]
+    scratch += [32 * NZ, 16 * NZ, 8 * NZ]
+    scratch += [16 * 64, 8 * 64, 8 * 32]
+    scratch += [table_rows(SIDES[NY]), table_rows(SIDES[NZ])]
+    scratch += [Y_ROWS] * 2 + [128] * 2 + [Z_ROWS] * 6
+    scratch += [128, 128, 256, 128, 64, 128, 64, 3 * 128, 6 * 64, 12 * 32] + [16] * 6
+    scratch += [512] * 2 + [X23_ROWS] * 2 + [64] * 2 + [16] * 4
+    operands = [velocity.reshape(NX * NY, NZ), *[jnp.asarray(matrix) for matrix in SPREADS], jnp.asarray(Z_SENDS)]
+    got = pl.pallas_call(
+        kernel,
+        out_shape=[jax.ShapeDtypeStruct((rows, 128), F32) for rows in results],
+        in_specs=[hbm] * 5,
+        out_specs=[vmem] * len(results),
+        scratch_shapes=[wide(rows) for rows in scratch]
+        + [pltpu.VMEM(matrix.shape, jnp.bfloat16) for matrix in SPREADS]
+        + [wide(32)]
+        + [pltpu.SemaphoreType.DMA((5,)), pltpu.SemaphoreType.DMA((14,)), pltpu.SemaphoreType.DMA((14,))],
+        compiler_params=pltpu.CompilerParams(collective_id=0, has_side_effects=True, vmem_limit_bytes=28 * 2**20),
+    )(*[pltpu.with_memory_space_constraint(a, pltpu.HBM) for a in operands])
     shapes = [(7 * 8 * 64, 128), (7 * 4 * 32, 64), (7 * 2 * 16, 32), (2 * 16, 32)]
     out1, out2, out3, out4 = pl.pallas_call(
-        kernel,
+        finish,
         out_shape=[jax.ShapeDtypeStruct(shape, F32) for shape in shapes],
-        in_specs=[pl.BlockSpec(memory_space=pl.ANY)],
-        out_specs=[pl.BlockSpec(memory_space=pltpu.VMEM)] * 4,
-        scratch_shapes=[pltpu.VMEM((rows, 128), F32) for rows in rows_of_scratch()]
-        + [pltpu.SemaphoreType.DMA, pltpu.SemaphoreType.DMA((10,)), pltpu.SemaphoreType.DMA((10,))],
-        compiler_params=pltpu.CompilerParams(collective_id=0, has_side_effects=True, vmem_limit_bytes=40 * 2**20),
-    )(velocity.reshape(NX * NY, NZ))
+        in_specs=[vmem] * len(results),
+        out_specs=[hbm] * 4,
+        scratch_shapes=[pltpu.VMEM(shape, F32) for shape in shapes] + [pltpu.SemaphoreType.DMA((10,))],
+        compiler_params=pltpu.CompilerParams(vmem_limit_bytes=16 * 2**20),
+    )(*got)
     return (
         out1.reshape(7, 8, 64, 128).transpose(0, 1, 3, 2),
         out2.reshape(7, 4, 32, 64).transpose(0, 1, 3, 2),

time: 33 us -> 28.1 us (0.85)
  local copies, waits for them, and re-layouts: 4.83 us -> 0 us
    unnamed x6 -> x0, local copies, waits for them, and re-layouts: 4.83 us -> none
    pallas_call x1 -> x2, Pallas kernels: 27.4 us -> 27.3 us  [the longest x1 25.1 us: shards(): pl.pallas_call(kernel, out_shape=[jax.ShapeDtypeStruct((rows, 128), F32)...]
where the time goes in v2:
time: 28.1 us; the launch traced here: 27.9 us
  Pallas kernels  27.3 us (97%)
  between operations  0.64 us (2%)
    pallas_call x1, Pallas kernels, shards(): pl.pallas_call(kernel, out_shape=[jax.ShapeDtypeStruct((rows, 128), F32)...  25.1 us
    pallas_call x1, Pallas kernels, shards(): pl.pallas_call(finish, out_shape=[jax.ShapeDtypeStruct(shape, F32) for sh...  2.17 us

profile of v2, /device:TPU:1, one launch (start us, length us, event | category | flops | bytes accessed | tf_op | source)
XLA Modules:
  0.0 27.9 jit_solution(8329284167347345158)
XLA Ops:
  0.6 25.1 %shard_map.84 = (f32[4096,128]{1,0:T(8,128)S(1)}, f32[1024,128]{1,0:T(8,128)S(1)}, f32[256,128]{1,0:T(8,128)S(1)}, f32[512,128]{1,0:T(8,128)S(1)}, f32[512,128]{...) custom-call(f32[4096,128]{1,0:T(8,128)} %bitcast.13, ...), custom_call_target="tpu_custom_call" | custom-call | tf_op jit(solution)/shard_map/pallas_call | solution.py:731
  25.8 2.2 %shard_map.85 = (f32[3584,128]{1,0:T(8,128)}, f32[896,64]{1,0:T(8,128)}, f32[224,32]{1,0:T(8,128)}, f32[32,32]{1,0:T(8,128)}) custom-call(f32[4096,128]{1,0:T(8,128)S(1)} %get-tuple-element.17.w1, f32[1024,128]{1,0:T(8,128)S(1)} %get-tuple-element.18.w2, f32[256,128]{1,0:T(8,128)S(1)} %get-tuple-element.19.w3, f32[512,128]{1,0:T(8,128)S(1)} %get-tuple-element.20.x1rl, ...), custom_call_target="tpu_custom_call" | custom-call | tf_op jit(solution)/shard_map/pallas_call | solution.py:743

commit v3 on v2

--- a/solution.py
+++ b/solution.py
@@ -367,7 +367,7 @@
             correct(ref, x * (NY >> level), SIDES[NY][level], y_places[level], ytab, own, lambda f: f * NX + x)
         return c
 
-    lax.fori_loop(0, NX, lift_y, 0)
+    lax.fori_loop(0, NX, lift_y, 0, unroll=2)
     pl.semaphore_wait(barrier, len(near))
     y_left = remote(0, ysl, yrr.at[pl.ds(0, Y_ROWS)], "yl")
     y_right = remote(1, ysr, yrl.at[pl.ds(0, Y_ROWS)], "yr")
@@ -384,8 +384,8 @@
         z3[pl.ds(p * 128, 128), :] = y3[pl.ds(p * 128, 128), :].T
         return c
 
-    lax.fori_loop(0, NX, turn, 0, unroll=2)
-    lax.fori_loop(0, NX // 2, turn_three, 0, unroll=2)
+    lax.fori_loop(0, NX, turn, 0, unroll=4)
+    lax.fori_loop(0, NX // 2, turn_three, 0, unroll=8)
 
     def z_sums(level, load_row, store):
         rows = {}
@@ -445,8 +445,8 @@
         lift_rows(z1, i * NZ, NZ, w1, i * NZ)
         return c
 
-    lax.fori_loop(0, NX // 2, lift_z3, 0)
-    lax.fori_loop(0, NX, lift_z2, 0)
+    lax.fori_loop(0, NX // 2, lift_z3, 0, unroll=4)
+    lax.fori_loop(0, NX, lift_z2, 0, unroll=4)
 
     y_left.wait()
     y_right.wait()
@@ -477,7 +477,7 @@
         for i, value in enumerate(slots(level, g[pl.ds(0, n), :], g[pl.ds(n, n), :])):
             p[pl.ds(n * i, n), :] = value
 
-    lax.fori_loop(0, 2 * NX, lift_z1, 0)
+    lax.fori_loop(0, 2 * NX, lift_z1, 0, unroll=4)
 
     def spread_one(x, c):
         keep = (lanes_of((128, 128)) & 15) == x
@@ -499,7 +499,7 @@
         w3[at, :] = w3[at, :] + expand(3, [p3[pl.ds(32 * i, 32), :] for i in range(12)], keep, spread3)
         return c
 
-    lax.fori_loop(0, NX, spread_one, 0)
+    lax.fori_loop(0, NX, spread_one, 0, unroll=4)
 
     def sums_one(g, c):
         rows = [w1[pl.ds(x * 256 + 8 * g, 8), :] for x in (0, 1, 2, 12, 13, 14, 15)]
@@ -513,8 +513,8 @@
     x1_right = remote(7, x1sr, x1rl, "xr")
     x1_left.start()
     x1_right.start()
-    lax.fori_loop(0, NX // 2, spread_three, 0)
-    lax.fori_loop(0, NX, spread_two, 0)
+    lax.fori_loop(0, NX // 2, spread_three, 0, unroll=8)
+    lax.fori_loop(0, NX, spread_two, 0, unroll=8)
 
     for copy in (z_left, z_right, zl_left, zl_right):
         copy.wait()
@@ -581,8 +581,8 @@
             correct(w1, x * 256 + 128 * t, SIDES[NZ][0], z_places[0], ztab, z_past, row_one(x, t))
         return c
 
-    lax.fori_loop(0, NX // 2, finish_z3, 0)
-    lax.fori_loop(0, NX, finish_z2, 0)
+    lax.fori_loop(0, NX // 2, finish_z3, 0, unroll=2)
+    lax.fori_loop(0, NX, finish_z2, 0, unroll=4)
 
     def sums_two(g, c):
         rows = [w2[pl.ds(x * 64 + 8 * g, 8), :] for x in range(NX)]
@@ -599,7 +599,7 @@
         return c
 
     lax.fori_loop(0, 8, sums_two, 0)
-    lax.fori_loop(0, 4, send_three, 0)
+    lax.fori_loop(0, 4, send_three, 0, unroll=2)
     x23_left = remote(10, x23sl, x23rr, "xl")
     x23_right = remote(11, x23sr, x23rl, "xr")
     x3_left = remote(12, x3sl, x3rr, "xll")

time: 28.1 us -> 24.3 us (0.86)
  Pallas kernels: 27.3 us -> 23.5 us
    pallas_call x1, Pallas kernels: 25.1 us -> 21.3 us  [shards(): pl.pallas_call(kernel, out_shape=[jax.ShapeDtypeStruct((rows, 128), F32)...]
where the time goes in v3:
time: 24.3 us; the launch traced here: 24.1 us
  Pallas kernels  23.5 us (97%)
  between operations  0.64 us (3%)
    pallas_call x1, Pallas kernels, shards(): pl.pallas_call(kernel, out_shape=[jax.ShapeDtypeStruct((rows, 128), F32)...  21.3 us
    pallas_call x1, Pallas kernels, shards(): pl.pallas_call(finish, out_shape=[jax.ShapeDtypeStruct(shape, F32) for sh...  2.17 us

profile of v3, /device:TPU:1, one launch (start us, length us, event | category | flops | bytes accessed | tf_op | source)
XLA Modules:
  0.0 24.1 jit_solution(6546507706429312553)
XLA Ops:
  0.6 21.3 %shard_map.84 = (f32[4096,128]{1,0:T(8,128)S(1)}, f32[1024,128]{1,0:T(8,128)S(1)}, f32[256,128]{1,0:T(8,128)S(1)}, f32[512,128]{1,0:T(8,128)S(1)}, f32[512,128]{...) custom-call(f32[4096,128]{1,0:T(8,128)} %bitcast.13, ...), custom_call_target="tpu_custom_call" | custom-call | tf_op jit(solution)/shard_map/pallas_call | solution.py:731
  22.0 2.2 %shard_map.85 = (f32[3584,128]{1,0:T(8,128)}, f32[896,64]{1,0:T(8,128)}, f32[224,32]{1,0:T(8,128)}, f32[32,32]{1,0:T(8,128)}) custom-call(f32[4096,128]{1,0:T(8,128)S(1)} %get-tuple-element.17.w1, f32[1024,128]{1,0:T(8,128)S(1)} %get-tuple-element.18.w2, f32[256,128]{1,0:T(8,128)S(1)} %get-tuple-element.19.w3, f32[512,128]{1,0:T(8,128)S(1)} %get-tuple-element.20.x1rl, ...), custom_call_target="tpu_custom_call" | custom-call | tf_op jit(solution)/shard_map/pallas_call | solution.py:743

commit v4 on v3

--- a/solution.py
+++ b/solution.py
@@ -276,9 +276,13 @@
 
 
 SPREADS = [spread(level) for level in (1, 2, 3)]
-Z_SENDS = np.zeros((32, NZ), np.float32)
+Z_SENDS = np.zeros((40, NZ), np.float32)
 for _at, _rows in enumerate((PLANS[NZ][2]["left"], PLANS[NZ][2]["right"], *MIRRORS)):
     Z_SENDS[8 * _at : 8 * _at + 6] = _rows
+for _at, _rows in enumerate((X_ONE["left"], X_ONE["right"])):
+    for _xf in range(2):
+        for _f in range(2):
+            Z_SENDS[32 + 4 * _at + 2 * _xf + _f, _f * NX : (_f + 1) * NX] = _rows[_xf]
 
 
 def split(value):
@@ -295,7 +299,8 @@
     lane = lanes_of(left.shape)
     turn = lambda value, by: pltpu.roll(value, by, 1)
     if level == 1:
-        one, two, three = split(jnp.where(lane < 32, left, jnp.where(lane < 64, turn(right, 32), 0.0)))
+        base = left if right is None else jnp.where(lane < 32, left, jnp.where(lane < 64, turn(right, 32), 0.0))
+        one, two, three = split(base)
         return [one + turn(one, 64), one + turn(two, 64), two + turn(three, 64)]
     if level == 2:
         one, two, three = split(jnp.where(lane < 64, left, turn(right, 64)))
@@ -311,7 +316,8 @@
 
 def kernel(
     vel, spread1_hbm, spread2_hbm, spread3_hbm, sends_hbm,
-    w1, w2, w3, x1rl, x1rr, x23rl, x23rr, x3rl, x3rr,
+    o1, o2, o3, o4,
+    w1, w2, w3, x1rl, x1rr, x23rl, x23rr, x3rl, x3rr, eg,
     v, y1, y2, y3, z1, z2, z3, t2, t3, t4, ytab, ztab,
     ysl, ysr, yrl, yrr, zsl, zsr, zrl, zrr, zml, zmr,
     htl, htr, g1, g2, g3, u2, u3, p1, p2, p3, zlsl, zlsr, zlrl, zlrr, zlml, zlmr,
@@ -338,6 +344,7 @@
     z_places = build_table(ztab, SIDES[NZ])
     for ref in (yrl, yrr):
         ref[pl.ds(Y_ROWS, 32), :] = jnp.zeros((32, 128), F32)
+    eg[...] = jnp.zeros((128, 128), F32)
 
     def remote(index, src, dst, to):
         return pltpu.make_async_remote_copy(
@@ -358,6 +365,12 @@
             ysl[pl.ds(f * NX + 8 * h, 8), :] = fir(SEND_LEFT[NY][f][:21], head)
             ysr[pl.ds(f * NX + 8 * h, 8), :] = fir(SEND_RIGHT[NY][f][-28:], tail)
 
+    pl.semaphore_wait(barrier, len(near))
+    y_left = remote(0, ysl, yrr.at[pl.ds(0, Y_ROWS)], "yl")
+    y_right = remote(1, ysr, yrl.at[pl.ds(0, Y_ROWS)], "yr")
+    y_left.start()
+    y_right.start()
+
     def lift_y(x, c):
         lift_rows(v, x * NY, NY, y1, x * NY)
         lift_rows(y1, x * NY, NY // 2, y2, x * (NY // 2))
@@ -368,24 +381,18 @@
         return c
 
     lax.fori_loop(0, NX, lift_y, 0, unroll=2)
-    pl.semaphore_wait(barrier, len(near))
-    y_left = remote(0, ysl, yrr.at[pl.ds(0, Y_ROWS)], "yl")
-    y_right = remote(1, ysr, yrl.at[pl.ds(0, Y_ROWS)], "yr")
-    y_left.start()
-    y_right.start()
-
-    def turn(x, c):
+    def turn_one(x, c):
         for t in range(2):
             z1[pl.ds(x * 256 + 128 * t, 128), :] = y1[pl.ds(x * NY + 128 * t, 128), :].T
+        return c
+
+    def turn_two(x, c):
         z2[pl.ds(x * 128, 128), :] = y2[pl.ds(x * 128, 128), :].T
         return c
 
     def turn_three(p, c):
         z3[pl.ds(p * 128, 128), :] = y3[pl.ds(p * 128, 128), :].T
         return c
-
-    lax.fori_loop(0, NX, turn, 0, unroll=4)
-    lax.fori_loop(0, NX // 2, turn_three, 0, unroll=8)
 
     def z_sums(level, load_row, store):
         rows = {}
@@ -401,6 +408,44 @@
                 ks = [k for k in range(NZ) if weights[k] != 0.0]
                 store(ref, f, fir([weights[k] for k in ks], [row(k) for k in ks]))
 
+    lax.fori_loop(0, NX // 2, turn_three, 0, unroll=8)
+    lax.fori_loop(0, NX, turn_two, 0, unroll=8)
+
+    def store_three(ref, f, value):
+        ref[pl.ds(Z_THREE + f * (NX // 2), 8), :] = value
+
+    z_sums(3, lambda k: z3[pl.ds(k, 8, stride=128), :], store_three)
+    for h in range(2):
+
+        def store_two(ref, f, value, h=h):
+            ref[pl.ds(Z_TWO + f * NX + 8 * h, 8), :] = value
+
+        z_sums(2, lambda k, h=h: z2[pl.ds(h * 8 * 128 + k, 8, stride=128), :], store_two)
+    deep = pl.ds(Z_TWO, Z_ROWS - Z_TWO)
+    z_left = remote(2, zsl.at[deep], zrr.at[deep], "zl")
+    z_right = remote(3, zsr.at[deep], zrl.at[deep], "zr")
+    z_left.start()
+    z_right.start()
+
+    def lift_z1(i, c):
+        lift_rows(z1, i * NZ, NZ, w1, i * NZ)
+        return c
+
+    lax.fori_loop(0, NX, turn_one, 0, unroll=4)
+    lax.fori_loop(0, 2 * NX, lift_z1, 0, unroll=4)
+
+    def sums_one(g, c):
+        rows = [w1[pl.ds(x * 256 + 8 * g, 8), :] for x in (0, 1, 2, 12, 13, 14, 15)]
+        for f in range(2):
+            x1sl[pl.ds(f * 256 + 8 * g, 8), :] = fir(X_ONE_LEFT[f][:3], rows[:3])
+            x1sr[pl.ds(f * 256 + 8 * g, 8), :] = fir(X_ONE_RIGHT[f][12:], rows[3:])
+        return c
+
+    lax.fori_loop(0, 32, sums_one, 0, unroll=4)
+    x1_left = remote(6, x1sl, x1rr, "xl")
+    x1_right = remote(7, x1sr, x1rl, "xr")
+    x1_left.start()
+    x1_right.start()
     for h in range(2):
         for t in range(2):
 
@@ -408,20 +453,11 @@
                 ref[pl.ds((f * 2 + t) * NX + 8 * h, 8), :] = value
 
             z_sums(1, lambda k, h=h, t=t: z1[pl.ds(h * 8 * 256 + t * 128 + k, 8, stride=256), :], store_one)
-
-        def store_two(ref, f, value, h=h):
-            ref[pl.ds(Z_TWO + f * NX + 8 * h, 8), :] = value
-
-        z_sums(2, lambda k, h=h: z2[pl.ds(h * 8 * 128 + k, 8, stride=128), :], store_two)
-
-    def store_three(ref, f, value):
-        ref[pl.ds(Z_THREE + f * (NX // 2), 8), :] = value
-
-    z_sums(3, lambda k: z3[pl.ds(k, 8, stride=128), :], store_three)
-    z_left = remote(2, zsl, zrr, "zl")
-    z_right = remote(3, zsr, zrl, "zr")
-    z_left.start()
-    z_right.start()
+    first = pl.ds(0, Z_TWO)
+    z1_left = remote(14, zsl.at[first], zrr.at[first], "zl")
+    z1_right = remote(15, zsr.at[first], zrl.at[first], "zr")
+    z1_left.start()
+    z1_right.start()
 
     row_one = lambda x, t: lambda f: (f * 2 + t) * NX + x
     row_two = lambda x: lambda f: Z_TWO + f * NX + x
@@ -440,13 +476,6 @@
         lift_rows(t4, p * 32, 32, w3, p * 32)
         correct(w3, p * 32, SIDES[NZ][2], z_places[2], ztab, z_own, row_three(p))
         return c
-
-    def lift_z1(i, c):
-        lift_rows(z1, i * NZ, NZ, w1, i * NZ)
-        return c
-
-    lax.fori_loop(0, NX // 2, lift_z3, 0, unroll=4)
-    lax.fori_loop(0, NX, lift_z2, 0, unroll=4)
 
     y_left.wait()
     y_right.wait()
@@ -455,13 +484,16 @@
     htl[...] = yrl[...].T
     htr[...] = yrr[...].T
     for at, ref in ((0, htl), (8, htr)):
-        sums = jnp.dot(sends[...], ref[...], precision=lax.Precision.HIGHEST, preferred_element_type=F32)
+        sums = jnp.dot(sends[pl.ds(0, 32), :], ref[...], precision=lax.Precision.HIGHEST, preferred_element_type=F32)
         for i, out in enumerate((zlsl, zlsr, zlml, zlmr)):
             out[pl.ds(at, 8), :] = sums[8 * i : 8 * i + 8]
     zl_left = remote(4, zlsl, zlrr, "zl")
     zl_right = remote(5, zlsr, zlrl, "zr")
     zl_left.start()
     zl_right.start()
+
+    lax.fori_loop(0, NX // 2, lift_z3, 0, unroll=4)
+    lax.fori_loop(0, NX, lift_z2, 0, unroll=4)
 
     for i, ref in enumerate((htl, htr)):
         lift_rows(ref, 0, 128, g1, 128 * i)
@@ -477,8 +509,6 @@
         for i, value in enumerate(slots(level, g[pl.ds(0, n), :], g[pl.ds(n, n), :])):
             p[pl.ds(n * i, n), :] = value
 
-    lax.fori_loop(0, 2 * NX, lift_z1, 0, unroll=4)
-
     def spread_one(x, c):
         keep = (lanes_of((128, 128)) & 15) == x
         value = expand(1, [p1[pl.ds(128 * i, 128), :] for i in range(3)], keep, spread1)
@@ -499,24 +529,10 @@
         w3[at, :] = w3[at, :] + expand(3, [p3[pl.ds(32 * i, 32), :] for i in range(12)], keep, spread3)
         return c
 
-    lax.fori_loop(0, NX, spread_one, 0, unroll=4)
-
-    def sums_one(g, c):
-        rows = [w1[pl.ds(x * 256 + 8 * g, 8), :] for x in (0, 1, 2, 12, 13, 14, 15)]
-        for f in range(2):
-            x1sl[pl.ds(f * 256 + 8 * g, 8), :] = fir(X_ONE_LEFT[f][:3], rows[:3])
-            x1sr[pl.ds(f * 256 + 8 * g, 8), :] = fir(X_ONE_RIGHT[f][12:], rows[3:])
-        return c
-
-    lax.fori_loop(0, 32, sums_one, 0, unroll=4)
-    x1_left = remote(6, x1sl, x1rr, "xl")
-    x1_right = remote(7, x1sr, x1rl, "xr")
-    x1_left.start()
-    x1_right.start()
     lax.fori_loop(0, NX // 2, spread_three, 0, unroll=8)
     lax.fori_loop(0, NX, spread_two, 0, unroll=8)
 
-    for copy in (z_left, z_right, zl_left, zl_right):
+    for copy in (z_left, z_right, z1_left, z1_right, zl_left, zl_right):
         copy.wait()
     gz = lax.axis_index("gz")
 
@@ -553,6 +569,19 @@
                     at = pl.ds((Z_TWO if level == 2 else Z_THREE) + f * count, count)
                     ref[at, :] = ref[at, :] + piece
 
+    sums = lax.dot_general(
+        sends[pl.ds(32, 8), :],
+        g1[...],
+        (((1,), (1,)), ((), ())),
+        precision=lax.Precision.HIGHEST,
+        preferred_element_type=F32,
+    )
+    for way, ref in enumerate((xesl, xesr)):
+        for xf in range(2):
+            for side in range(2):
+                at = 4 * way + 2 * xf
+                ref[pl.ds(16 + 4 * xf + 2 * side, 2), :] = sums[at : at + 2, 128 * side : 128 * side + 128]
+
     for side, ref in enumerate((zrl, zrr)):
         for f in range(2):
             for t in range(2):
@@ -606,44 +635,27 @@
     x3_right = remote(13, x3sr, x3rl, "xrr")
     for copy in (x23_left, x23_right, x3_left, x3_right):
         copy.start()
+    lax.fori_loop(0, NX, spread_one, 0, unroll=4)
     lax.fori_loop(0, NX, finish_z1, 0)
     for copy in (x1_left, x1_right, xe_left, xe_right):
         copy.wait()
+    for side, ends in enumerate((xerl, xerr)):
+        for xf in range(2):
+            for h in range(4):
+                eg[pl.ds(NX * h + 2 * side + xf, 1), :] = ends[pl.ds(16 + 4 * xf + h, 1), :]
+    arrays = slots(1, eg[...].T, None)
+    for side, ref in enumerate((x1rl, x1rr)):
+        for xf in range(2):
+            value = expand(1, arrays, (lanes_of((128, 128)) & 15) == 2 * side + xf, spread1)
+            for t in range(2):
+                at = pl.ds(xf * 256 + 128 * t, 128)
+                ref[at, :] = ref[at, :] + value[:, 128 * t : 128 * t + 128]
     for xf in range(2):
         for t in range(2):
             for ref, ends in ((x1rl, xerl), (x1rr, xerr)):
                 at = (xf * 2 + t) * 4
                 refs = {"from_left": ends.at[pl.ds(at, 2)], "from_right": ends.at[pl.ds(at + 2, 2)]}
                 correct(ref, xf * 256 + 128 * t, SIDES[NZ][0], z_places[0], ztab, refs, lambda f: f)
-    for copy in (x23_left, x23_right, x3_left, x3_right):
-        copy.wait()
-
-
-def paired(weights, rows):
-    low_lanes = lanes_of((8, 128)) < 64
-    total = jnp.zeros((8, 128), F32)
-    for p in range(NX // 2):
-        if weights[2 * p] == 0.0 and weights[2 * p + 1] == 0.0:
-            continue
-        total = total + jnp.where(low_lanes, weights[2 * p], weights[2 * p + 1]) * rows[p]
-    return total + pltpu.roll(total, 64, 1)
-
-
-def sums_three(matrix, rows):
-    low_lanes = lanes_of((8, 128)) < 64
-    return [jnp.where(low_lanes, paired(matrix[2 * h], rows), paired(matrix[2 * h + 1], rows)) for h in range(2)]
-
-
-def finish(w1, w2, w3, x1rl, x1rr, x23rl, x23rr, x3rl, x3rr, out1, out2, out3, out4, o1, o2, o3, o4, sems):
-    lane = lanes_of((8, 128))
-    low_lanes = lane < 64
-    copies = []
-
-    def send(src, dst):
-        copy = pltpu.make_async_copy(src, dst, sems.at[len(copies)])
-        copy.start()
-        copies.append(copy)
-
     for hy in range(2):
         for hz in range(2):
 
@@ -662,12 +674,11 @@
                     o1[pl.ds((band - 1) * 512 + (i % 8) * 64 + 8 * g, 8), :] = value
                 return c
 
-            lax.fori_loop(0, 8, out_one, 0)
-            for hx in range(2):
-                band = 4 * hx + 2 * hy + hz
-                if band:
-                    at = pl.ds((band - 1) * 512, 512)
-                    send(o1.at[at], out1.at[at])
+            lax.fori_loop(0, 8, out_one, 0, unroll=2)
+    for copy in (x23_left, x23_right, x3_left, x3_right):
+        copy.wait()
+    lane = lanes_of((8, 128))
+    low_lanes = lane < 64
 
     def out_two(g, hz):
         rows = [w2[pl.ds(x * 64 + 8 * g, 8), :] for x in range(NX)]
@@ -686,7 +697,6 @@
 
     for g in range(8):
         out_two(g, g // 4)
-    send(o2, out2)
 
     def out_three(g, hz):
         rows = [w3[pl.ds(p * 32 + 8 * g, 8), :] for p in range(NX // 2)]
@@ -710,8 +720,31 @@
 
     for g in range(4):
         out_three(g, g // 2)
-    send(o3, out3)
-    send(o4, out4)
+
+
+def paired(weights, rows):
+    low_lanes = lanes_of((8, 128)) < 64
+    total = jnp.zeros((8, 128), F32)
+    for p in range(NX // 2):
+        if weights[2 * p] == 0.0 and weights[2 * p + 1] == 0.0:
+            continue
+        total = total + jnp.where(low_lanes, weights[2 * p], weights[2 * p + 1]) * rows[p]
+    return total + pltpu.roll(total, 64, 1)
+
+
+def sums_three(matrix, rows):
+    low_lanes = lanes_of((8, 128)) < 64
+    return [jnp.where(low_lanes, paired(matrix[2 * h], rows), paired(matrix[2 * h + 1], rows)) for h in range(2)]
+
+
+def write(o1, o2, o3, o4, out1, out2, out3, out4, sems):
+    copies = []
+    for src, dst, parts in ((o1, out1, 7), (o2, out2, 1), (o3, out3, 1), (o4, out4, 1)):
+        rows = src.shape[0] // parts
+        for i in range(parts):
+            at = pl.ds(i * rows, rows)
+            copies.append(pltpu.make_async_copy(src.at[at], dst.at[at], sems.at[len(copies)]))
+            copies[-1].start()
     for copy in copies:
         copy.wait()
 
@@ -719,33 +752,33 @@
 def shards(velocity):
     vmem, hbm = pl.BlockSpec(memory_space=pltpu.VMEM), pl.BlockSpec(memory_space=pltpu.HBM)
     wide = lambda rows: pltpu.VMEM((rows, 128), F32)
-    results = [32 * NZ, 16 * 64, 8 * 32, 512, 512, X23_ROWS, X23_ROWS, 64, 64]
-    scratch = [16 * NY, 16 * NY, 16 * NY // 2, 16 * NY // 4]
+    shapes = [(7 * 8 * 64, 128), (7 * 4 * 32, 64), (7 * 2 * 16, 32), (2 * 16, 32)]
+    scratch = [32 * NZ, 16 * 64, 8 * 32, 512, 512, X23_ROWS, X23_ROWS, 64, 64, 128]
+    scratch += [16 * NY, 16 * NY, 16 * NY // 2, 16 * NY // 4]
     scratch += [32 * NZ, 16 * NZ, 8 * NZ]
     scratch += [16 * 64, 8 * 64, 8 * 32]
     scratch += [table_rows(SIDES[NY]), table_rows(SIDES[NZ])]
     scratch += [Y_ROWS] * 2 + [128] * 2 + [Z_ROWS] * 6
     scratch += [128, 128, 256, 128, 64, 128, 64, 3 * 128, 6 * 64, 12 * 32] + [16] * 6
-    scratch += [512] * 2 + [X23_ROWS] * 2 + [64] * 2 + [16] * 4
+    scratch += [512] * 2 + [X23_ROWS] * 2 + [64] * 2 + [24] * 4
     operands = [velocity.reshape(NX * NY, NZ), *[jnp.asarray(matrix) for matrix in SPREADS], jnp.asarray(Z_SENDS)]
     got = pl.pallas_call(
         kernel,
-        out_shape=[jax.ShapeDtypeStruct((rows, 128), F32) for rows in results],
+        out_shape=[jax.ShapeDtypeStruct(shape, F32) for shape in shapes],
         in_specs=[hbm] * 5,
-        out_specs=[vmem] * len(results),
+        out_specs=[vmem] * 4,
         scratch_shapes=[wide(rows) for rows in scratch]
         + [pltpu.VMEM(matrix.shape, jnp.bfloat16) for matrix in SPREADS]
-        + [wide(32)]
-        + [pltpu.SemaphoreType.DMA((5,)), pltpu.SemaphoreType.DMA((14,)), pltpu.SemaphoreType.DMA((14,))],
+        + [wide(40)]
+        + [pltpu.SemaphoreType.DMA((5,)), pltpu.SemaphoreType.DMA((16,)), pltpu.SemaphoreType.DMA((16,))],
         compiler_params=pltpu.CompilerParams(collective_id=0, has_side_effects=True, vmem_limit_bytes=28 * 2**20),
     )(*[pltpu.with_memory_space_constraint(a, pltpu.HBM) for a in operands])
-    shapes = [(7 * 8 * 64, 128), (7 * 4 * 32, 64), (7 * 2 * 16, 32), (2 * 16, 32)]
     out1, out2, out3, out4 = pl.pallas_call(
-        finish,
+        write,
         out_shape=[jax.ShapeDtypeStruct(shape, F32) for shape in shapes],
-        in_specs=[vmem] * len(results),
+        in_specs=[vmem] * 4,
         out_specs=[hbm] * 4,
-        scratch_shapes=[pltpu.VMEM(shape, F32) for shape in shapes] + [pltpu.SemaphoreType.DMA((10,))],
+        scratch_shapes=[pltpu.SemaphoreType.DMA((10,))],
         compiler_params=pltpu.CompilerParams(vmem_limit_bytes=16 * 2**20),
     )(*got)
     return (

time: 24.3 us -> 23 us (0.947)
  Pallas kernels: 23.5 us -> 22.3 us
    pallas_call x2, Pallas kernels: 23.5 us -> 22.3 us  [the longest x1 20.8 us: shards(): pl.pallas_call(kernel, out_shape=[jax.ShapeDtypeStruct(shape, F32) for sh...]
where the time goes in v4:
time: 23 us; the launch traced here: 22.9 us
  Pallas kernels  22.3 us (97%)
  between operations  0.64 us (3%)
    pallas_call x1, Pallas kernels, shards(): pl.pallas_call(kernel, out_shape=[jax.ShapeDtypeStruct(shape, F32) for sh...  20.8 us
    pallas_call x1, Pallas kernels, shards(): pl.pallas_call(write, out_shape=[jax.ShapeDtypeStruct(shape, F32) for sha...  1.49 us

profile of v4, /device:TPU:1, one launch (start us, length us, event | category | flops | bytes accessed | tf_op | source)
XLA Modules:
  0.0 22.9 jit_solution(17752135525167537865)
XLA Ops:
  0.6 20.8 %shard_map.84 = (f32[3584,128]{1,0:T(8,128)S(1)}, f32[896,64]{1,0:T(8,128)S(1)}, f32[224,32]{1,0:T(8,128)S(1)}, f32[32,32]{1,0:T(8,128)S(1)}) custom-call(f32[4096,128]{1,0:T(8,128)} %bitcast.13, bf16[384,256]{1,0:T(8,128)(2,1)} %constant.8.clone.spread1_hbm, bf16[768,128]{1,0:T(8,128)(2,1)} %constant.9.clone.spread2_hbm, ...), custom_call_target="tpu_custom_call" | custom-call | tf_op jit(solution)/shard_map/pallas_call | solution.py:765
  21.4 1.5 %shard_map.85 = (f32[3584,128]{1,0:T(8,128)}, f32[896,64]{1,0:T(8,128)}, f32[224,32]{1,0:T(8,128)}, f32[32,32]{1,0:T(8,128)}) custom-call(f32[3584,128]{1,0:T(8,128)S(1)} %get-tuple-element.12.o1, f32[896,64]{1,0:T(8,128)S(1)} %get-tuple-element.13.o2, f32[224,32]{1,0:T(8,128)S(1)} %get-tuple-element.14.o3, f32[32,32]{1,0:T(8,128)S(1)} %get-tuple-element.15.o4), custom_call_target="tpu_custom_call" | custom-call | tf_op jit(solution)/shard_map/pallas_call | solution.py:776

commit v5 on v4

--- a/solution.py
+++ b/solution.py
@@ -251,7 +251,7 @@
 
 def parts_of(value):
     rest, parts = np.asarray(value, np.float32), []
-    for _ in range(3):
+    for _ in range(2):
         part = rest.astype(ml_dtypes.bfloat16)
         parts.append(part)
         rest = rest - part.astype(np.float32)
@@ -271,8 +271,8 @@
         matrix = np.concatenate(blocks)
     else:
         matrix = np.repeat(np.concatenate([left, right]), NX, axis=0)
-    one, two, three = parts_of(matrix)
-    return np.concatenate([one, two, three, one, two, one])
+    one, two = parts_of(matrix)
+    return np.concatenate([one, two, one, two])
 
 
 SPREADS = [spread(level) for level in (1, 2, 3)]
@@ -284,11 +284,9 @@
         for _f in range(2):
             Z_SENDS[32 + 4 * _at + 2 * _xf + _f, _f * NX : (_f + 1) * NX] = _rows[_xf]
 
-
 def split(value):
     one = value.astype(jnp.bfloat16).astype(F32)
-    two = (value - one).astype(jnp.bfloat16).astype(F32)
-    return one, two, value - one - two
+    return one, value - one
 
 
 def lanes_of(shape):
@@ -300,13 +298,13 @@
     turn = lambda value, by: pltpu.roll(value, by, 1)
     if level == 1:
         base = left if right is None else jnp.where(lane < 32, left, jnp.where(lane < 64, turn(right, 32), 0.0))
-        one, two, three = split(base)
-        return [one + turn(one, 64), one + turn(two, 64), two + turn(three, 64)]
+        one, two = split(base)
+        return [one + turn(one, 64), two + turn(two, 64)]
     if level == 2:
-        one, two, three = split(jnp.where(lane < 64, left, turn(right, 64)))
-        return [one, one, one, two, two, three]
-    one, two, three = zip(split(left), split(right))
-    return [*one, *one, *one, *two, *two, *three]
+        one, two = split(jnp.where(lane < 64, left, turn(right, 64)))
+        return [one, one, two, two]
+    one, two = zip(split(left), split(right))
+    return [*one, *one, *two, *two]
 
 
 def expand(level, arrays, keep, spread_ref):
@@ -320,9 +318,9 @@
     w1, w2, w3, x1rl, x1rr, x23rl, x23rr, x3rl, x3rr, eg,
     v, y1, y2, y3, z1, z2, z3, t2, t3, t4, ytab, ztab,
     ysl, ysr, yrl, yrr, zsl, zsr, zrl, zrr, zml, zmr,
-    htl, htr, g1, g2, g3, u2, u3, p1, p2, p3, zlsl, zlsr, zlrl, zlrr, zlml, zlmr,
+    htl, htr, g1, g2, g3, u2, u3, p1, p2, p3, csl, csr, zlsl, zlsr, zlml, zlmr,
     x1sl, x1sr, x23sl, x23sr, x3sl, x3sr, xesl, xesr, xerl, xerr,
-    spread1, spread2, spread3, sends,
+    spread1, spread2, spread3, sends, zc, zf, q2, q3,
     load_sems, send_sems, recv_sems,
 ):
     loads = [
@@ -342,7 +340,7 @@
         pl.semaphore_signal(barrier, inc=1, device_id=device, device_id_type=MESH)
     y_places = build_table(ytab, SIDES[NY])
     z_places = build_table(ztab, SIDES[NZ])
-    for ref in (yrl, yrr):
+    for ref in (yrl, yrr, ysl, ysr):
         ref[pl.ds(Y_ROWS, 32), :] = jnp.zeros((32, 128), F32)
     eg[...] = jnp.zeros((128, 128), F32)
 
@@ -365,9 +363,22 @@
             ysl[pl.ds(f * NX + 8 * h, 8), :] = fir(SEND_LEFT[NY][f][:21], head)
             ysr[pl.ds(f * NX + 8 * h, 8), :] = fir(SEND_RIGHT[NY][f][-28:], tail)
 
+    loads[1].wait()
+    for at, ref in enumerate((ysl, ysr)):
+        sums = jnp.dot(
+            sends[pl.ds(0, 16), :], ref[...].T, precision=lax.Precision.HIGHEST, preferred_element_type=F32
+        )
+        csl[pl.ds(8 * at, 8), :] = sums[:8]
+        csr[pl.ds(8 * at, 8), :] = sums[8:]
+    corners = []
+    for at in range(2):
+        corners.append(remote(4 + at, csl.at[pl.ds(8 * at, 8)], zc.at[pl.ds(16 * at, 8)], "zl"))
+        corners.append(remote(16 + at, csr.at[pl.ds(8 * at, 8)], zc.at[pl.ds(16 * at + 8, 8)], "zr"))
     pl.semaphore_wait(barrier, len(near))
-    y_left = remote(0, ysl, yrr.at[pl.ds(0, Y_ROWS)], "yl")
-    y_right = remote(1, ysr, yrl.at[pl.ds(0, Y_ROWS)], "yr")
+    for copy in corners:
+        copy.start()
+    y_left = remote(0, ysl.at[pl.ds(0, Y_ROWS)], yrr.at[pl.ds(0, Y_ROWS)], "yl")
+    y_right = remote(1, ysr.at[pl.ds(0, Y_ROWS)], yrl.at[pl.ds(0, Y_ROWS)], "yr")
     y_left.start()
     y_right.start()
 
@@ -432,6 +443,12 @@
         return c
 
     lax.fori_loop(0, NX, turn_one, 0, unroll=4)
+    for copy in corners:
+        copy.wait()
+    zf_left = remote(18, zc.at[pl.ds(0, 16)], zf.at[pl.ds(0, 16)], "yl")
+    zf_right = remote(19, zc.at[pl.ds(16, 16)], zf.at[pl.ds(16, 16)], "yr")
+    zf_left.start()
+    zf_right.start()
     lax.fori_loop(0, 2 * NX, lift_z1, 0, unroll=4)
 
     def sums_one(g, c):
@@ -477,9 +494,12 @@
         correct(w3, p * 32, SIDES[NZ][2], z_places[2], ztab, z_own, row_three(p))
         return c
 
+    lax.fori_loop(0, NX // 2, lift_z3, 0, unroll=4)
+    lax.fori_loop(0, NX, lift_z2, 0, unroll=4)
+
     y_left.wait()
     y_right.wait()
-    for load in loads[1:]:
+    for load in loads[2:]:
         load.wait()
     htl[...] = yrl[...].T
     htr[...] = yrr[...].T
@@ -487,14 +507,6 @@
         sums = jnp.dot(sends[pl.ds(0, 32), :], ref[...], precision=lax.Precision.HIGHEST, preferred_element_type=F32)
         for i, out in enumerate((zlsl, zlsr, zlml, zlmr)):
             out[pl.ds(at, 8), :] = sums[8 * i : 8 * i + 8]
-    zl_left = remote(4, zlsl, zlrr, "zl")
-    zl_right = remote(5, zlsr, zlrl, "zr")
-    zl_left.start()
-    zl_right.start()
-
-    lax.fori_loop(0, NX // 2, lift_z3, 0, unroll=4)
-    lax.fori_loop(0, NX, lift_z2, 0, unroll=4)
-
     for i, ref in enumerate((htl, htr)):
         lift_rows(ref, 0, 128, g1, 128 * i)
         lift_rows(g1, 128 * i, 64, u2, 64 * i)
@@ -509,66 +521,6 @@
         for i, value in enumerate(slots(level, g[pl.ds(0, n), :], g[pl.ds(n, n), :])):
             p[pl.ds(n * i, n), :] = value
 
-    def spread_one(x, c):
-        keep = (lanes_of((128, 128)) & 15) == x
-        value = expand(1, [p1[pl.ds(128 * i, 128), :] for i in range(3)], keep, spread1)
-        for t in range(2):
-            at = pl.ds(x * 256 + 128 * t, 128)
-            w1[at, :] = w1[at, :] + value[:, 128 * t : 128 * t + 128]
-        return c
-
-    def spread_two(x, c):
-        keep = (lanes_of((64, 128)) & 15) == x
-        at = pl.ds(x * 64, 64)
-        w2[at, :] = w2[at, :] + expand(2, [p2[pl.ds(64 * i, 64), :] for i in range(6)], keep, spread2)
-        return c
-
-    def spread_three(p, c):
-        keep = ((lanes_of((32, 128)) & 15) >> 1) == p
-        at = pl.ds(p * 32, 32)
-        w3[at, :] = w3[at, :] + expand(3, [p3[pl.ds(32 * i, 32), :] for i in range(12)], keep, spread3)
-        return c
-
-    lax.fori_loop(0, NX // 2, spread_three, 0, unroll=8)
-    lax.fori_loop(0, NX, spread_two, 0, unroll=8)
-
-    for copy in (z_left, z_right, z1_left, z1_right, zl_left, zl_right):
-        copy.wait()
-    gz = lax.axis_index("gz")
-
-    @pl.when(gz == 0)
-    def _():
-        zrl[...] = zml[...]
-        zlrl[...] = zlml[...]
-
-    @pl.when(gz == SIZES["gz"] - 1)
-    def _():
-        zrr[...] = zmr[...]
-        zlrr[...] = zlmr[...]
-
-    lane, sub = lanes_of((16, 128)), lax.broadcasted_iota(jnp.int32, (16, 128), 0)
-    for late, ref in ((zlrl, zrl), (zlrr, zrr)):
-        left, right = late[pl.ds(0, 8), :], late[pl.ds(8, 8), :]
-        for level, spread_ref, count in ((3, spread3, 8), (2, spread2, NX), (1, spread1, NX)):
-            arrays = slots(level, left, right)
-            if level == 3:
-                keep = ((lane[:8] & 15) >> 1) == sub[:8]
-            else:
-                keep = (lane & 15) == sub
-            tall = [
-                jnp.concatenate([jnp.where(keep, a[f : f + 1], 0.0) for f in range(2 * level)], axis=0) for a in arrays
-            ]
-            value = expand(level, tall, jnp.full(tall[0].shape, True), spread_ref)
-            for f in range(2 * level):
-                piece = value[f * count : f * count + count]
-                if level == 1:
-                    for t in range(2):
-                        at = pl.ds((f * 2 + t) * NX, NX)
-                        ref[at, :] = ref[at, :] + piece[:, 128 * t : 128 * t + 128]
-                else:
-                    at = pl.ds((Z_TWO if level == 2 else Z_THREE) + f * count, count)
-                    ref[at, :] = ref[at, :] + piece
-
     sums = lax.dot_general(
         sends[pl.ds(32, 8), :],
         g1[...],
@@ -581,6 +533,89 @@
             for side in range(2):
                 at = 4 * way + 2 * xf
                 ref[pl.ds(16 + 4 * xf + 2 * side, 2), :] = sums[at : at + 2, 128 * side : 128 * side + 128]
+    xg_left = remote(20, xesl.at[pl.ds(16, 8)], xerr.at[pl.ds(16, 8)], "xl")
+    xg_right = remote(21, xesr.at[pl.ds(16, 8)], xerl.at[pl.ds(16, 8)], "xr")
+    xg_left.start()
+    xg_right.start()
+
+    def spread_one(x, c):
+        keep = (lanes_of((128, 128)) & 15) == x
+        value = expand(1, [p1[pl.ds(128 * i, 128), :] for i in range(2)], keep, spread1)
+        for t in range(2):
+            at = pl.ds(x * 256 + 128 * t, 128)
+            w1[at, :] = w1[at, :] + value[:, 128 * t : 128 * t + 128]
+        return c
+
+    def spread_two(x, c):
+        keep = (lanes_of((64, 128)) & 15) == x
+        at = pl.ds(x * 64, 64)
+        w2[at, :] = w2[at, :] + expand(2, [p2[pl.ds(64 * i, 64), :] for i in range(4)], keep, spread2)
+        return c
+
+    def spread_three(p, c):
+        keep = ((lanes_of((32, 128)) & 15) >> 1) == p
+        at = pl.ds(p * 32, 32)
+        w3[at, :] = w3[at, :] + expand(3, [p3[pl.ds(32 * i, 32), :] for i in range(8)], keep, spread3)
+        return c
+
+    lax.fori_loop(0, NX // 2, spread_three, 0, unroll=8)
+    lax.fori_loop(0, NX, spread_two, 0, unroll=8)
+
+    for copy in (z_left, z_right, zf_left, zf_right):
+        copy.wait()
+    gz = lax.axis_index("gz")
+
+    @pl.when(gz == 0)
+    def _():
+        zrl[deep, :] = zml[deep, :]
+        zf[pl.ds(24, 8), :] = zlml[pl.ds(0, 8), :]
+        zf[pl.ds(8, 8), :] = zlml[pl.ds(8, 8), :]
+
+    @pl.when(gz == SIZES["gz"] - 1)
+    def _():
+        zrr[deep, :] = zmr[deep, :]
+        zf[pl.ds(16, 8), :] = zlmr[pl.ds(0, 8), :]
+        zf[pl.ds(0, 8), :] = zlmr[pl.ds(8, 8), :]
+
+    def complete(level):
+        lane, sub = lanes_of((16, 128)), lax.broadcasted_iota(jnp.int32, (16, 128), 0)
+        count = NX // 2 if level == 3 else NX
+        keep = ((lane[:8] & 15) >> 1) == sub[:8] if level == 3 else (lane & 15) == sub
+        tall = []
+        for at in (8, 0):
+            arrays = slots(level, zf[pl.ds(16 + at, 8), :], zf[pl.ds(at, 8), :])
+            tall.append([
+                jnp.concatenate([jnp.where(keep, a[f : f + 1], 0.0) for f in range(2 * level)], axis=0) for a in arrays
+            ])
+        both = [jnp.concatenate(pair, axis=0) for pair in zip(*tall)]
+        value = expand(level, both, jnp.full(both[0].shape, True), (spread1, spread2, spread3)[level - 1])
+        for side, ref in enumerate((zrl, zrr)):
+            for f in range(2 * level):
+                first_row = (side * 2 * level + f) * count
+                piece = value[first_row : first_row + count]
+                if level == 1:
+                    for t in range(2):
+                        at = pl.ds((f * 2 + t) * NX, NX)
+                        ref[at, :] = ref[at, :] + piece[:, 128 * t : 128 * t + 128]
+                else:
+                    at = pl.ds((Z_TWO if level == 2 else Z_THREE) + f * count, count)
+                    ref[at, :] = ref[at, :] + piece
+
+    complete(3)
+    complete(2)
+
+    for copy in (z1_left, z1_right):
+        copy.wait()
+
+    @pl.when(gz == 0)
+    def _():
+        zrl[first, :] = zml[first, :]
+
+    @pl.when(gz == SIZES["gz"] - 1)
+    def _():
+        zrr[first, :] = zmr[first, :]
+
+    complete(1)
 
     for side, ref in enumerate((zrl, zrr)):
         for f in range(2):
@@ -590,8 +625,8 @@
                     at = pl.ds((xf * 2 + t) * 4 + side * 2 + f, 1)
                     xesl[at, :] = fir(X_ONE_LEFT[xf][:3], rows[:3])
                     xesr[at, :] = fir(X_ONE_RIGHT[xf][12:], rows[3:])
-    xe_left = remote(8, xesl, xerr, "xl")
-    xe_right = remote(9, xesr, xerl, "xr")
+    xe_left = remote(8, xesl.at[pl.ds(0, 16)], xerr.at[pl.ds(0, 16)], "xl")
+    xe_right = remote(9, xesr.at[pl.ds(0, 16)], xerl.at[pl.ds(0, 16)], "xr")
     xe_left.start()
     xe_right.start()
 
@@ -605,13 +640,10 @@
         correct(w3, p * 32, SIDES[NZ][2], z_places[2], ztab, z_past, row_three(p))
         return c
 
-    def finish_z1(x, c):
-        for t in range(2):
-            correct(w1, x * 256 + 128 * t, SIDES[NZ][0], z_places[0], ztab, z_past, row_one(x, t))
-        return c
-
-    lax.fori_loop(0, NX // 2, finish_z3, 0, unroll=2)
+    lax.fori_loop(0, NX // 2, finish_z3, 0, unroll=4)
     lax.fori_loop(0, NX, finish_z2, 0, unroll=4)
+
+    three_to = ((x23sr, N_TWO * 64), (x23sl, N_TWO * 64), (x3sr, 0), (x3sl, 0))
 
     def sums_two(g, c):
         rows = [w2[pl.ds(x * 64 + 8 * g, 8), :] for x in range(NX)]
@@ -622,12 +654,12 @@
 
     def send_three(g, c):
         rows = [w3[pl.ds(p * 32 + 8 * g, 8), :] for p in range(NX // 2)]
-        for ref, block, at in ((x23sr, 1, N_TWO * 64), (x23sl, 3, N_TWO * 64), (x3sr, 0, 0), (x3sl, 4, 0)):
+        for (ref, at), block in zip(three_to, (1, 3, 0, 4)):
             for h, value in enumerate(sums_three(X_THREE[block], rows)):
                 ref[pl.ds(at + 32 * h + 8 * g, 8), :] = value
         return c
 
-    lax.fori_loop(0, 8, sums_two, 0)
+    lax.fori_loop(0, 8, sums_two, 0, unroll=2)
     lax.fori_loop(0, 4, send_three, 0, unroll=2)
     x23_left = remote(10, x23sl, x23rr, "xl")
     x23_right = remote(11, x23sr, x23rl, "xr")
@@ -635,9 +667,29 @@
     x3_right = remote(13, x3sr, x3rl, "xrr")
     for copy in (x23_left, x23_right, x3_left, x3_right):
         copy.start()
+
+    def finish_z1(x, c):
+        for t in range(2):
+            correct(w1, x * 256 + 128 * t, SIDES[NZ][0], z_places[0], ztab, z_past, row_one(x, t))
+        return c
+
     lax.fori_loop(0, NX, spread_one, 0, unroll=4)
     lax.fori_loop(0, NX, finish_z1, 0)
-    for copy in (x1_left, x1_right, xe_left, xe_right):
+    def own_two(g, c):
+        rows = [w2[pl.ds(x * 64 + 8 * g, 8), :] for x in range(NX)]
+        for i in range(8):
+            q2[pl.ds(i * 64 + 8 * g, 8), :] = fir(X_TWO_OWN[i], rows)
+        return c
+
+    def own_three(g, c):
+        rows = [w3[pl.ds(p * 32 + 8 * g, 8), :] for p in range(NX // 2)]
+        for h, value in enumerate(sums_three(X_THREE[2], rows)):
+            q3[pl.ds(32 * h + 8 * g, 8), :] = value
+        return c
+
+    lax.fori_loop(0, 8, own_two, 0, unroll=2)
+    lax.fori_loop(0, 4, own_three, 0, unroll=2)
+    for copy in (x1_left, x1_right, xg_left, xg_right, xe_left, xe_right):
         copy.wait()
     for side, ends in enumerate((xerl, xerr)):
         for xf in range(2):
@@ -681,12 +733,12 @@
     low_lanes = lane < 64
 
     def out_two(g, hz):
-        rows = [w2[pl.ds(x * 64 + 8 * g, 8), :] for x in range(NX)]
         left = [x23rl[pl.ds(f * 64 + 8 * g, 8), :] for f in range(N_TWO)]
         right = [x23rr[pl.ds(f * 64 + 8 * g, 8), :] for f in range(N_TWO)]
         for i in range(8):
             hx = i // 4
-            value = fir(X_TWO_OWN[i] + X_TWO_FROM_LEFT[i] + X_TWO_FROM_RIGHT[i], rows + left + right)
+            own = q2[pl.ds(i * 64 + 8 * g, 8), :]
+            value = fir([1.0] + X_TWO_FROM_LEFT[i] + X_TWO_FROM_RIGHT[i], [own] + left + right)
             scale = SCALES[1][hx] * SCALES[1][hz]
             value = value * jnp.where(low_lanes, scale * SCALES[1][0], scale * SCALES[1][1])
             for hy in range(2):
@@ -699,11 +751,9 @@
         out_two(g, g // 4)
 
     def out_three(g, hz):
-        rows = [w3[pl.ds(p * 32 + 8 * g, 8), :] for p in range(NX // 2)]
-        own = sums_three(X_THREE[2], rows)
         high_y = (lane & 63) >= 32
         for hx in range(2):
-            value = own[hx]
+            value = q3[pl.ds(32 * hx + 8 * g, 8), :]
             for ref, at in ((x23rl, N_TWO * 64), (x23rr, N_TWO * 64), (x3rl, 0), (x3rr, 0)):
                 value = value + ref[pl.ds(at + 32 * hx + 8 * g, 8), :]
             scale = SCALES[2][hx] * SCALES[2][hz]
@@ -758,8 +808,8 @@
     scratch += [32 * NZ, 16 * NZ, 8 * NZ]
     scratch += [16 * 64, 8 * 64, 8 * 32]
     scratch += [table_rows(SIDES[NY]), table_rows(SIDES[NZ])]
-    scratch += [Y_ROWS] * 2 + [128] * 2 + [Z_ROWS] * 6
-    scratch += [128, 128, 256, 128, 64, 128, 64, 3 * 128, 6 * 64, 12 * 32] + [16] * 6
+    scratch += [128] * 4 + [Z_ROWS] * 6
+    scratch += [128, 128, 256, 128, 64, 128, 64, 2 * 128, 4 * 64, 8 * 32] + [16] * 6
     scratch += [512] * 2 + [X23_ROWS] * 2 + [64] * 2 + [24] * 4
     operands = [velocity.reshape(NX * NY, NZ), *[jnp.asarray(matrix) for matrix in SPREADS], jnp.asarray(Z_SENDS)]
     got = pl.pallas_call(
@@ -769,8 +819,8 @@
         out_specs=[vmem] * 4,
         scratch_shapes=[wide(rows) for rows in scratch]
         + [pltpu.VMEM(matrix.shape, jnp.bfloat16) for matrix in SPREADS]
-        + [wide(40)]
-        + [pltpu.SemaphoreType.DMA((5,)), pltpu.SemaphoreType.DMA((16,)), pltpu.SemaphoreType.DMA((16,))],
+        + [wide(rows) for rows in (40, 32, 32, 512, 64)]
+        + [pltpu.SemaphoreType.DMA((5,)), pltpu.SemaphoreType.DMA((22,)), pltpu.SemaphoreType.DMA((22,))],
         compiler_params=pltpu.CompilerParams(collective_id=0, has_side_effects=True, vmem_limit_bytes=28 * 2**20),
     )(*[pltpu.with_memory_space_constraint(a, pltpu.HBM) for a in operands])
     out1, out2, out3, out4 = pl.pallas_call(

time: 23 us -> 22.5 us (0.978)
  Pallas kernels: 22.3 us -> 21.8 us
    pallas_call x1, Pallas kernels: 20.8 us -> 20.3 us  [shards(): pl.pallas_call(kernel, out_shape=[jax.ShapeDtypeStruct(shape, F32) for sh...]
where the time goes in v5:
time: 22.5 us; the launch traced here: 22.4 us
  Pallas kernels  21.8 us (97%)
  between operations  0.64 us (3%)
    pallas_call x1, Pallas kernels, shards(): pl.pallas_call(kernel, out_shape=[jax.ShapeDtypeStruct(shape, F32) for sh...  20.3 us
    pallas_call x1, Pallas kernels, shards(): pl.pallas_call(write, out_shape=[jax.ShapeDtypeStruct(shape, F32) for sha...  1.49 us

profile of v5, /device:TPU:1, one launch (start us, length us, event | category | flops | bytes accessed | tf_op | source)
XLA Modules:
  0.0 22.4 jit_solution(18063423718421009163)
XLA Ops:
  0.6 20.3 %shard_map.84 = (f32[3584,128]{1,0:T(8,128)S(1)}, f32[896,64]{1,0:T(8,128)S(1)}, f32[224,32]{1,0:T(8,128)S(1)}, f32[32,32]{1,0:T(8,128)S(1)}) custom-call(f32[4096,128]{1,0:T(8,128)} %bitcast.13, bf16[256,256]{1,0:T(8,128)(2,1)} %constant.8.clone.spread1_hbm, bf16[512,128]{1,0:T(8,128)(2,1)} %constant.9.clone.spread2_hbm, ...), custom_call_target="tpu_custom_call" | custom-call | tf_op jit(solution)/shard_map/pallas_call | solution.py:815
  20.9 1.5 %shard_map.85 = (f32[3584,128]{1,0:T(8,128)}, f32[896,64]{1,0:T(8,128)}, f32[224,32]{1,0:T(8,128)}, f32[32,32]{1,0:T(8,128)}) custom-call(f32[3584,128]{1,0:T(8,128)S(1)} %get-tuple-element.12.o1, f32[896,64]{1,0:T(8,128)S(1)} %get-tuple-element.13.o2, f32[224,32]{1,0:T(8,128)S(1)} %get-tuple-element.14.o3, f32[32,32]{1,0:T(8,128)S(1)} %get-tuple-element.15.o4), custom_call_target="tpu_custom_call" | custom-call | tf_op jit(solution)/shard_map/pallas_call | solution.py:826

commit v6 on v5

--- a/solution.py
+++ b/solution.py
@@ -420,7 +420,7 @@
                 store(ref, f, fir([weights[k] for k in ks], [row(k) for k in ks]))
 
     lax.fori_loop(0, NX // 2, turn_three, 0, unroll=8)
-    lax.fori_loop(0, NX, turn_two, 0, unroll=8)
+    lax.fori_loop(0, NX, turn_two, 0, unroll=16)
 
     def store_three(ref, f, value):
         ref[pl.ds(Z_THREE + f * (NX // 2), 8), :] = value
@@ -442,14 +442,15 @@
         lift_rows(z1, i * NZ, NZ, w1, i * NZ)
         return c
 
-    lax.fori_loop(0, NX, turn_one, 0, unroll=4)
+    lax.fori_loop(0, NX, turn_one, 0, unroll=8)
     for copy in corners:
         copy.wait()
     zf_left = remote(18, zc.at[pl.ds(0, 16)], zf.at[pl.ds(0, 16)], "yl")
     zf_right = remote(19, zc.at[pl.ds(16, 16)], zf.at[pl.ds(16, 16)], "yr")
     zf_left.start()
     zf_right.start()
-    lax.fori_loop(0, 2 * NX, lift_z1, 0, unroll=4)
+    lax.fori_loop(0, 6, lift_z1, 0, unroll=6)
+    lax.fori_loop(24, 32, lift_z1, 0, unroll=4)
 
     def sums_one(g, c):
         rows = [w1[pl.ds(x * 256 + 8 * g, 8), :] for x in (0, 1, 2, 12, 13, 14, 15)]
@@ -559,7 +560,7 @@
         return c
 
     lax.fori_loop(0, NX // 2, spread_three, 0, unroll=8)
-    lax.fori_loop(0, NX, spread_two, 0, unroll=8)
+    lax.fori_loop(0, NX, spread_two, 0, unroll=16)
 
     for copy in (z_left, z_right, zf_left, zf_right):
         copy.wait()
@@ -640,8 +641,8 @@
         correct(w3, p * 32, SIDES[NZ][2], z_places[2], ztab, z_past, row_three(p))
         return c
 
-    lax.fori_loop(0, NX // 2, finish_z3, 0, unroll=4)
-    lax.fori_loop(0, NX, finish_z2, 0, unroll=4)
+    lax.fori_loop(0, NX // 2, finish_z3, 0, unroll=8)
+    lax.fori_loop(0, NX, finish_z2, 0, unroll=16)
 
     three_to = ((x23sr, N_TWO * 64), (x23sl, N_TWO * 64), (x3sr, 0), (x3sl, 0))
 
@@ -659,8 +660,8 @@
                 ref[pl.ds(at + 32 * h + 8 * g, 8), :] = value
         return c
 
-    lax.fori_loop(0, 8, sums_two, 0, unroll=2)
-    lax.fori_loop(0, 4, send_three, 0, unroll=2)
+    lax.fori_loop(0, 8, sums_two, 0, unroll=8)
+    lax.fori_loop(0, 4, send_three, 0, unroll=4)
     x23_left = remote(10, x23sl, x23rr, "xl")
     x23_right = remote(11, x23sr, x23rl, "xr")
     x3_left = remote(12, x3sl, x3rr, "xll")
@@ -673,6 +674,7 @@
             correct(w1, x * 256 + 128 * t, SIDES[NZ][0], z_places[0], ztab, z_past, row_one(x, t))
         return c
 
+    lax.fori_loop(6, 24, lift_z1, 0, unroll=6)
     lax.fori_loop(0, NX, spread_one, 0, unroll=4)
     lax.fori_loop(0, NX, finish_z1, 0)
     def own_two(g, c):

time: 22.5 us -> 21.8 us (0.969)
  Pallas kernels: 21.8 us -> 21 us
    pallas_call x1, Pallas kernels: 20.3 us -> 19.5 us  [shards(): pl.pallas_call(kernel, out_shape=[jax.ShapeDtypeStruct(shape, F32) for sh...]
where the time goes in v6:
time: 21.8 us; the launch traced here: 21.6 us
  Pallas kernels  21 us (96%)
  between operations  0.64 us (3%)
    pallas_call x1, Pallas kernels, shards(): pl.pallas_call(kernel, out_shape=[jax.ShapeDtypeStruct(shape, F32) for sh...  19.5 us
    pallas_call x1, Pallas kernels, shards(): pl.pallas_call(write, out_shape=[jax.ShapeDtypeStruct(shape, F32) for sha...  1.49 us

profile of v6, /device:TPU:1, one launch (start us, length us, event | category | flops | bytes accessed | tf_op | source)
XLA Modules:
  0.0 21.6 jit_solution(2789619166080553226)
XLA Ops:
  0.6 19.5 %shard_map.84 = (f32[3584,128]{1,0:T(8,128)S(1)}, f32[896,64]{1,0:T(8,128)S(1)}, f32[224,32]{1,0:T(8,128)S(1)}, f32[32,32]{1,0:T(8,128)S(1)}) custom-call(f32[4096,128]{1,0:T(8,128)} %bitcast.13, bf16[256,256]{1,0:T(8,128)(2,1)} %constant.8.clone.spread1_hbm, bf16[512,128]{1,0:T(8,128)(2,1)} %constant.9.clone.spread2_hbm, ...), custom_call_target="tpu_custom_call" | custom-call | tf_op jit(solution)/shard_map/pallas_call | solution.py:817
  20.1 1.5 %shard_map.85 = (f32[3584,128]{1,0:T(8,128)}, f32[896,64]{1,0:T(8,128)}, f32[224,32]{1,0:T(8,128)}, f32[32,32]{1,0:T(8,128)}) custom-call(f32[3584,128]{1,0:T(8,128)S(1)} %get-tuple-element.12.o1, f32[896,64]{1,0:T(8,128)S(1)} %get-tuple-element.13.o2, f32[224,32]{1,0:T(8,128)S(1)} %get-tuple-element.14.o3, f32[32,32]{1,0:T(8,128)S(1)} %get-tuple-element.15.o4), custom_call_target="tpu_custom_call" | custom-call | tf_op jit(solution)/shard_map/pallas_call | solution.py:828

commit v7 on v6

--- a/solution.py
+++ b/solution.py
@@ -314,13 +314,13 @@
 
 def kernel(
     vel, spread1_hbm, spread2_hbm, spread3_hbm, sends_hbm,
-    o1, o2, o3, o4,
-    w1, w2, w3, x1rl, x1rr, x23rl, x23rr, x3rl, x3rr, eg,
+    o1, q2, q3, x23rl, x23rr, x3rl, x3rr,
+    w1, w2, w3, x1rl, x1rr, eg,
     v, y1, y2, y3, z1, z2, z3, t2, t3, t4, ytab, ztab,
     ysl, ysr, yrl, yrr, zsl, zsr, zrl, zrr, zml, zmr,
     htl, htr, g1, g2, g3, u2, u3, p1, p2, p3, csl, csr, zlsl, zlsr, zlml, zlmr,
     x1sl, x1sr, x23sl, x23sr, x3sl, x3sr, xesl, xesr, xerl, xerr,
-    spread1, spread2, spread3, sends, zc, zf, q2, q3,
+    spread1, spread2, spread3, sends, zc, zf,
     load_sems, send_sems, recv_sems,
 ):
     loads = [
@@ -731,26 +731,35 @@
             lax.fori_loop(0, 8, out_one, 0, unroll=2)
     for copy in (x23_left, x23_right, x3_left, x3_right):
         copy.wait()
+
+
+def paired(weights, rows):
+    low_lanes = lanes_of((8, 128)) < 64
+    total = jnp.zeros((8, 128), F32)
+    for p in range(NX // 2):
+        if weights[2 * p] == 0.0 and weights[2 * p + 1] == 0.0:
+            continue
+        total = total + jnp.where(low_lanes, weights[2 * p], weights[2 * p + 1]) * rows[p]
+    return total + pltpu.roll(total, 64, 1)
+
+
+def sums_three(matrix, rows):
+    low_lanes = lanes_of((8, 128)) < 64
+    return [jnp.where(low_lanes, paired(matrix[2 * h], rows), paired(matrix[2 * h + 1], rows)) for h in range(2)]
+
+
+def write(o1, q2, q3, x23rl, x23rr, x3rl, x3rr, out1, out2, out3, out4, o2, o3, o4, sems):
+    copies = []
+
+    def send(src, dst):
+        copies.append(pltpu.make_async_copy(src, dst, sems.at[len(copies)]))
+        copies[-1].start()
+
+    for band in range(7):
+        at = pl.ds(band * 512, 512)
+        send(o1.at[at], out1.at[at])
     lane = lanes_of((8, 128))
     low_lanes = lane < 64
-
-    def out_two(g, hz):
-        left = [x23rl[pl.ds(f * 64 + 8 * g, 8), :] for f in range(N_TWO)]
-        right = [x23rr[pl.ds(f * 64 + 8 * g, 8), :] for f in range(N_TWO)]
-        for i in range(8):
-            hx = i // 4
-            own = q2[pl.ds(i * 64 + 8 * g, 8), :]
-            value = fir([1.0] + X_TWO_FROM_LEFT[i] + X_TWO_FROM_RIGHT[i], [own] + left + right)
-            scale = SCALES[1][hx] * SCALES[1][hz]
-            value = value * jnp.where(low_lanes, scale * SCALES[1][0], scale * SCALES[1][1])
-            for hy in range(2):
-                band = 4 * hx + 2 * hy + hz
-                if band:
-                    at = (band - 1) * 128 + (i % 4) * 32 + 8 * (g % 4)
-                    o2[pl.ds(at, 8), :] = value[:, 64 * hy : 64 * hy + 64]
-
-    for g in range(8):
-        out_two(g, g // 4)
 
     def out_three(g, hz):
         high_y = (lane & 63) >= 32
@@ -772,31 +781,27 @@
 
     for g in range(4):
         out_three(g, g // 2)
-
-
-def paired(weights, rows):
-    low_lanes = lanes_of((8, 128)) < 64
-    total = jnp.zeros((8, 128), F32)
-    for p in range(NX // 2):
-        if weights[2 * p] == 0.0 and weights[2 * p + 1] == 0.0:
-            continue
-        total = total + jnp.where(low_lanes, weights[2 * p], weights[2 * p + 1]) * rows[p]
-    return total + pltpu.roll(total, 64, 1)
-
-
-def sums_three(matrix, rows):
-    low_lanes = lanes_of((8, 128)) < 64
-    return [jnp.where(low_lanes, paired(matrix[2 * h], rows), paired(matrix[2 * h + 1], rows)) for h in range(2)]
-
-
-def write(o1, o2, o3, o4, out1, out2, out3, out4, sems):
-    copies = []
-    for src, dst, parts in ((o1, out1, 7), (o2, out2, 1), (o3, out3, 1), (o4, out4, 1)):
-        rows = src.shape[0] // parts
-        for i in range(parts):
-            at = pl.ds(i * rows, rows)
-            copies.append(pltpu.make_async_copy(src.at[at], dst.at[at], sems.at[len(copies)]))
-            copies[-1].start()
+    send(o3, out3)
+    send(o4, out4)
+
+    def out_two(g, hz):
+        left = [x23rl[pl.ds(f * 64 + 8 * g, 8), :] for f in range(N_TWO)]
+        right = [x23rr[pl.ds(f * 64 + 8 * g, 8), :] for f in range(N_TWO)]
+        for i in range(8):
+            hx = i // 4
+            own = q2[pl.ds(i * 64 + 8 * g, 8), :]
+            value = fir([1.0] + X_TWO_FROM_LEFT[i] + X_TWO_FROM_RIGHT[i], [own] + left + right)
+            scale = SCALES[1][hx] * SCALES[1][hz]
+            value = value * jnp.where(low_lanes, scale * SCALES[1][0], scale * SCALES[1][1])
+            for hy in range(2):
+                band = 4 * hx + 2 * hy + hz
+                if band:
+                    at = (band - 1) * 128 + (i % 4) * 32 + 8 * (g % 4)
+                    o2[pl.ds(at, 8), :] = value[:, 64 * hy : 64 * hy + 64]
+
+    for g in range(8):
+        out_two(g, g // 4)
+    send(o2, out2)
     for copy in copies:
         copy.wait()
 
@@ -805,7 +810,8 @@
     vmem, hbm = pl.BlockSpec(memory_space=pltpu.VMEM), pl.BlockSpec(memory_space=pltpu.HBM)
     wide = lambda rows: pltpu.VMEM((rows, 128), F32)
     shapes = [(7 * 8 * 64, 128), (7 * 4 * 32, 64), (7 * 2 * 16, 32), (2 * 16, 32)]
-    scratch = [32 * NZ, 16 * 64, 8 * 32, 512, 512, X23_ROWS, X23_ROWS, 64, 64, 128]
+    results = [7 * 8 * 64, 512, 64, X23_ROWS, X23_ROWS, 64, 64]
+    scratch = [32 * NZ, 16 * 64, 8 * 32, 512, 512, 128]
     scratch += [16 * NY, 16 * NY, 16 * NY // 2, 16 * NY // 4]
     scratch += [32 * NZ, 16 * NZ, 8 * NZ]
     scratch += [16 * 64, 8 * 64, 8 * 32]
@@ -816,21 +822,21 @@
     operands = [velocity.reshape(NX * NY, NZ), *[jnp.asarray(matrix) for matrix in SPREADS], jnp.asarray(Z_SENDS)]
     got = pl.pallas_call(
         kernel,
-        out_shape=[jax.ShapeDtypeStruct(shape, F32) for shape in shapes],
+        out_shape=[jax.ShapeDtypeStruct((rows, 128), F32) for rows in results],
         in_specs=[hbm] * 5,
-        out_specs=[vmem] * 4,
+        out_specs=[vmem] * len(results),
         scratch_shapes=[wide(rows) for rows in scratch]
         + [pltpu.VMEM(matrix.shape, jnp.bfloat16) for matrix in SPREADS]
-        + [wide(rows) for rows in (40, 32, 32, 512, 64)]
+        + [wide(rows) for rows in (40, 32, 32)]
         + [pltpu.SemaphoreType.DMA((5,)), pltpu.SemaphoreType.DMA((22,)), pltpu.SemaphoreType.DMA((22,))],
         compiler_params=pltpu.CompilerParams(collective_id=0, has_side_effects=True, vmem_limit_bytes=28 * 2**20),
     )(*[pltpu.with_memory_space_constraint(a, pltpu.HBM) for a in operands])
     out1, out2, out3, out4 = pl.pallas_call(
         write,
         out_shape=[jax.ShapeDtypeStruct(shape, F32) for shape in shapes],
-        in_specs=[vmem] * 4,
+        in_specs=[vmem] * len(results),
         out_specs=[hbm] * 4,
-        scratch_shapes=[pltpu.SemaphoreType.DMA((10,))],
+        scratch_shapes=[pltpu.VMEM(shape, F32) for shape in shapes[1:]] + [pltpu.SemaphoreType.DMA((10,))],
         compiler_params=pltpu.CompilerParams(vmem_limit_bytes=16 * 2**20),
     )(*got)
     return (

time: 21.8 us -> 21.6 us (level)
  no operation moved by 1% of the time
where the time goes in v7:
time: 21.6 us; the launch traced here: 21.5 us
  Pallas kernels  20.8 us (96%)
  between operations  0.64 us (3%)
    pallas_call x1, Pallas kernels, shards(): pl.pallas_call(kernel, out_shape=[jax.ShapeDtypeStruct((rows, 128), F32)...  19.3 us
    pallas_call x1, Pallas kernels, shards(): pl.pallas_call(write, out_shape=[jax.ShapeDtypeStruct(shape, F32) for sha...  1.52 us

profile of v7, /device:TPU:1, one launch (start us, length us, event | category | flops | bytes accessed | tf_op | source)
XLA Modules:
  0.0 21.5 jit_solution(13835007656156107163)
XLA Ops:
  0.6 19.3 %shard_map.84 = (f32[3584,128]{1,0:T(8,128)S(1)}, f32[512,128]{1,0:T(8,128)S(1)}, f32[64,128]{1,0:T(8,128)S(1)}, f32[256,128]{1,0:T(8,128)S(1)}, f32[256,128]{1,...) custom-call(f32[4096,128]{1,0:T(8,128)} %bitcast.13, bf16[256,256]{1,0:T(8,128)(2,1)} %constant.8.clone.spread1_hbm, ...), custom_call_target="tpu_custom_call" | custom-call | tf_op jit(solution)/shard_map/pallas_call | solution.py:823
  20.0 1.5 %shard_map.85 = (f32[3584,128]{1,0:T(8,128)}, f32[896,64]{1,0:T(8,128)}, f32[224,32]{1,0:T(8,128)}, f32[32,32]{1,0:T(8,128)}) custom-call(f32[3584,128]{1,0:T(8,128)S(1)} %get-tuple-element.15.o1, f32[512,128]{1,0:T(8,128)S(1)} %get-tuple-element.16.q2, f32[64,128]{1,0:T(8,128)S(1)} %get-tuple-element.17.q3, f32[256,128]{1,0:T(8,128)S(1)} %get-tuple-element.18.x23rl, ...), custom_call_target="tpu_custom_call" | custom-call | tf_op jit(solution)/shard_map/pallas_call | solution.py:834

commit v8 on v7

--- a/solution.py
+++ b/solution.py
@@ -201,6 +201,8 @@
 X_TWO_FROM_RIGHT, X_TWO_LEFT = factored(X_TWO_BLOCKS[3])
 X_TWO_OWN = rounded(X_TWO_BLOCKS[2])
 X_THREE = [rounded(block) for block in line_blocks(NX, 3)]
+X_FAR_FROM_LEFT, X_FAR_RIGHT = factored(line_blocks(NX, 3)[0])
+X_FAR_FROM_RIGHT, X_FAR_LEFT = factored(line_blocks(NX, 3)[4])
 N_TWO = len(X_TWO_RIGHT)
 
 Y_ROWS = 6 * NX
@@ -644,7 +646,7 @@
     lax.fori_loop(0, NX // 2, finish_z3, 0, unroll=8)
     lax.fori_loop(0, NX, finish_z2, 0, unroll=16)
 
-    three_to = ((x23sr, N_TWO * 64), (x23sl, N_TWO * 64), (x3sr, 0), (x3sl, 0))
+    three_to = ((x23sr, N_TWO * 64), (x23sl, N_TWO * 64))
 
     def sums_two(g, c):
         rows = [w2[pl.ds(x * 64 + 8 * g, 8), :] for x in range(NX)]
@@ -655,9 +657,12 @@
 
     def send_three(g, c):
         rows = [w3[pl.ds(p * 32 + 8 * g, 8), :] for p in range(NX // 2)]
-        for (ref, at), block in zip(three_to, (1, 3, 0, 4)):
+        for (ref, at), block in zip(three_to, (1, 3)):
             for h, value in enumerate(sums_three(X_THREE[block], rows)):
                 ref[pl.ds(at + 32 * h + 8 * g, 8), :] = value
+        low_lanes = lanes_of((8, 128)) < 64
+        for ref, sums in ((x3sr, X_FAR_RIGHT), (x3sl, X_FAR_LEFT)):
+            ref[pl.ds(8 * g, 8), :] = jnp.where(low_lanes, paired(sums[0], rows), paired(sums[-1], rows))
         return c
 
     lax.fori_loop(0, 8, sums_two, 0, unroll=8)
@@ -765,8 +770,13 @@
         high_y = (lane & 63) >= 32
         for hx in range(2):
             value = q3[pl.ds(32 * hx + 8 * g, 8), :]
-            for ref, at in ((x23rl, N_TWO * 64), (x23rr, N_TWO * 64), (x3rl, 0), (x3rr, 0)):
-                value = value + ref[pl.ds(at + 32 * hx + 8 * g, 8), :]
+            for ref in (x23rl, x23rr):
+                value = value + ref[pl.ds(N_TWO * 64 + 32 * hx + 8 * g, 8), :]
+            for ref, uses in ((x3rl, X_FAR_FROM_LEFT), (x3rr, X_FAR_FROM_RIGHT)):
+                far, (low, high) = ref[pl.ds(8 * g, 8), :], uses[2 * hx : 2 * hx + 2]
+                value = value + jnp.where(low_lanes, low[0], high[-1]) * far
+                if len(low) == 2:
+                    value = value + jnp.where(low_lanes, low[1], high[0]) * pltpu.roll(far, 64, 1)
             scale = SCALES[2][hx] * SCALES[2][hz]
             value = value * jnp.where(high_y, scale * SCALES[2][1], scale * SCALES[2][0])
             for q in range(4):
@@ -810,7 +820,7 @@
     vmem, hbm = pl.BlockSpec(memory_space=pltpu.VMEM), pl.BlockSpec(memory_space=pltpu.HBM)
     wide = lambda rows: pltpu.VMEM((rows, 128), F32)
     shapes = [(7 * 8 * 64, 128), (7 * 4 * 32, 64), (7 * 2 * 16, 32), (2 * 16, 32)]
-    results = [7 * 8 * 64, 512, 64, X23_ROWS, X23_ROWS, 64, 64]
+    results = [7 * 8 * 64, 512, 64, X23_ROWS, X23_ROWS, 32, 32]
     scratch = [32 * NZ, 16 * 64, 8 * 32, 512, 512, 128]
     scratch += [16 * NY, 16 * NY, 16 * NY // 2, 16 * NY // 4]
     scratch += [32 * NZ, 16 * NZ, 8 * NZ]
@@ -818,7 +828,7 @@
     scratch += [table_rows(SIDES[NY]), table_rows(SIDES[NZ])]
     scratch += [128] * 4 + [Z_ROWS] * 6
     scratch += [128, 128, 256, 128, 64, 128, 64, 2 * 128, 4 * 64, 8 * 32] + [16] * 6
-    scratch += [512] * 2 + [X23_ROWS] * 2 + [64] * 2 + [24] * 4
+    scratch += [512] * 2 + [X23_ROWS] * 2 + [32] * 2 + [24] * 4
     operands = [velocity.reshape(NX * NY, NZ), *[jnp.asarray(matrix) for matrix in SPREADS], jnp.asarray(Z_SENDS)]
     got = pl.pallas_call(
         kernel,

time: 21.6 us -> 21.7 us (level)
  no operation moved by 1% of the time
where the time goes in v8:
time: 21.7 us; the launch traced here: 21.6 us
  Pallas kernels  20.9 us (96%)
  between operations  0.64 us (3%)
    pallas_call x1, Pallas kernels, shards(): pl.pallas_call(kernel, out_shape=[jax.ShapeDtypeStruct((rows, 128), F32)...  19.3 us
    pallas_call x1, Pallas kernels, shards(): pl.pallas_call(write, out_shape=[jax.ShapeDtypeStruct(shape, F32) for sha...  1.61 us

profile of v8, /device:TPU:1, one launch (start us, length us, event | category | flops | bytes accessed | tf_op | source)
XLA Modules:
  0.0 21.6 jit_solution(1051766326452605823)
XLA Ops:
  0.6 19.3 %shard_map.84 = (f32[3584,128]{1,0:T(8,128)S(1)}, f32[512,128]{1,0:T(8,128)S(1)}, f32[64,128]{1,0:T(8,128)S(1)}, f32[256,128]{1,0:T(8,128)S(1)}, f32[256,128]{1,...) custom-call(f32[4096,128]{1,0:T(8,128)} %bitcast.13, bf16[256,256]{1,0:T(8,128)(2,1)} %constant.8.clone.spread1_hbm, ...), custom_call_target="tpu_custom_call" | custom-call | tf_op jit(solution)/shard_map/pallas_call | solution.py:833
  20.0 1.6 %shard_map.85 = (f32[3584,128]{1,0:T(8,128)}, f32[896,64]{1,0:T(8,128)}, f32[224,32]{1,0:T(8,128)}, f32[32,32]{1,0:T(8,128)}) custom-call(f32[3584,128]{1,0:T(8,128)S(1)} %get-tuple-element.15.o1, f32[512,128]{1,0:T(8,128)S(1)} %get-tuple-element.16.q2, f32[64,128]{1,0:T(8,128)S(1)} %get-tuple-element.17.q3, f32[256,128]{1,0:T(8,128)S(1)} %get-tuple-element.18.x23rl, ...), custom_call_target="tpu_custom_call" | custom-call | tf_op jit(solution)/shard_map/pallas_call | solution.py:844
